TPU v7x, 256 devices: a whole 4x4x8 slice. The times are simulated.
256 devices in a mesh: mem: 8 (over x, core), band: 32 (over y, z).
Axes of the slice: x: 4, y: 4, z: 8, core: 2. Of those that a mesh axis runs over, the one named last changes fastest.
Arguments:
- control: bfloat16 [128, 2, 1536, 768], P('mem', None, 'band'), may hold values from -11 to 11
- member_pert: bfloat16 [128, 65536], P('mem', 'band'), may hold values from -6 to 6
- obs_weight: float32 [65536], P('band'), may hold values from 0.5 to 2
- obs_band: int32 [65536, 1], P('band'), may hold values from 0 to 31; in each aligned block of 2048 rows (0 to 2047, 2048 to 4095, ...) at most 128 rows name the same one
- obs_cell: int32 [65536], P('band'), may hold values from 0 to 73727
- length_x: float32 [2], replicated, may hold values from 30 to 120
- length_y: float32 [2], replicated, may hold values from 30 to 120
Outputs:
- gradient: float32 [128, 2, 1536, 768], P('mem', None, 'band')
- gradient_dot: float32 [], replicated
Inputs may be any that keep to these rules, and one draw needn't show every extreme that they name: `obs_band`: in each aligned block of 2048 rows (the rows of one band), at most 128 rows name the same band.
All inputs are finite; a program needn't handle non-finite values.
Results may differ from a plain program's by a relative error of at most 0.024.
Values may be sent and summed in bfloat16 or wider, within the bound.
No kernel may reach another device: no remote copies, remote signals or barrier semaphores. Data moves between devices by JAX's collectives and lax.ppermute only.
A program may use at most 192 MiB of HBM per device.

v0:
```python
import jax
import jax.numpy as jnp
from jax import lax
from jax.sharding import PartitionSpec as P


def joined(value, axis, join):
    pieces = jax.tree.map(lambda part: lax.all_gather(part, axis), value)
    head = jax.tree.map(lambda part: part[0], pieces)
    tail = jax.tree.map(lambda part: part[1:], pieces)
    subtotal, _ = lax.scan(lambda subtotal, share: (join(subtotal, share), None), head, tail)
    return subtotal


def kernels(lengths, length_n, periodic):
    offset = jnp.arange(length_n, dtype=jnp.int32)
    spread = jnp.abs(offset[:, None] - offset[None, :]).astype(jnp.float32)
    if periodic:
        spread = jnp.minimum(spread, length_n - spread)
    scale = 2.0 / jnp.sqrt(lengths)
    return (scale[:, None, None] * jnp.exp(-spread[None, :, :] / lengths[:, None, None])).astype(
        jnp.bfloat16
    )


def two_sum_add(first, second):
    high_a, low_a = first
    high_b, low_b = second
    summed = high_a + high_b
    back_part = summed - high_a
    error = high_a - (summed - back_part) + (high_b - back_part)
    return (summed, low_a + low_b + error)


def on_device(control, member_pert, obs_weight, obs_band, obs_cell, length_x, length_y):
    members, levels, x_block, ny_all = control.shape
    band_count = lax.axis_size("band")
    ny_loc = ny_all // band_count
    nx_all = x_block * band_count
    cell_count = levels * ny_loc * nx_all
    target = obs_band[:, 0]
    filter_x = kernels(length_x, nx_all, True)
    filter_y = kernels(length_y, ny_all, False)
    payload = obs_weight[None, :] * member_pert.astype(jnp.float32)
    placed = (target * cell_count + obs_cell).astype(jnp.float32)[None, :]
    got_values, got_placed = (
        lax.all_gather(payload, "band", axis=1, tiled=True),
        lax.all_gather(placed, "band", axis=1, tiled=True),
    )
    placed_int = got_placed[0].astype(jnp.int32)
    owner_band = placed_int // cell_count
    cell_at = placed_int - owner_band * cell_count
    values = jnp.where((owner_band == lax.axis_index("band"))[None, :], got_values, 0.0)
    grid_sum = jnp.zeros((members, cell_count), jnp.float32).at[:, cell_at].add(values)
    grid_sum = grid_sum.reshape(members, levels, ny_loc, nx_all).astype(jnp.bfloat16)
    zonal = jnp.einsum(
        "klyx,lxw->klyw", grid_sum, filter_x, preferred_element_type=jnp.float32
    ).astype(jnp.bfloat16)
    filtered = jnp.einsum(
        "klax,lya->klxy",
        lax.all_to_all(zonal, "band", split_axis=3, concat_axis=2, tiled=True),
        filter_y,
        preferred_element_type=jnp.float32,
    )
    gradient = control.astype(jnp.float32) + filtered
    partial_value = jnp.sum(gradient * gradient)
    high_part, low_part = joined(
        (partial_value, jnp.zeros((), jnp.float32)), ("mem", "band"), two_sum_add
    )
    summed = high_part + low_part
    all_members = members * lax.axis_size("mem")
    gradient_dot = summed * (1.0 / (all_members * levels * ny_all * nx_all))
    return (gradient, gradient_dot)


def solution(mesh):
    return jax.shard_map(
        on_device,
        mesh=mesh,
        in_specs=(
            P("mem", None, "band", None),
            P("mem", "band"),
            P("band"),
            P("band", None),
            P("band"),
            P(),
            P(),
        ),
        out_specs=(P("mem", None, "band", None), P()),
        check_vma=False,
    )
```

profile of v0, /device:TPU:1, one launch (start us, length us, event | category | flops | bytes accessed | tf_op | source)
XLA Modules:
  0.0 2111.6 jit_solution(4873921986217063238)
XLA Ops:
  7.2 1.5 convert_multiply_fusion
  8.7 0.7 broadcast_multiply_fusion
  9.5 0.7 add_convert_fusion
  10.2 42.4 %all-gather = f32[65536]{0:T(1024)S(1)} all-gather(f32[2048]{0:T(1024)S(1)} %add_convert_fusion), channel_id=2, replica_groups=mesh['mem'=8,'band'=32] {'band'}, dimensions={0}, use_global_device_ids=true | all-gather | bytes 270336 | tf_op jit(solution)/shard_map/all_gather | solution.py:48
  52.9 5.8 fusion.7
  58.6 1.1 compare_reduce_fusion
  59.7 1.7 compare_select_fusion
  61.5 32.7 %all-gather.3.cloned.1.call-done = f32[16,65536]{1,0:T(8,128)} async-done(((f32[16,2048]{1,0:T(8,128)}), f32[16,65536]{1,0:T(8,128)}) %all-gather.3.cloned.1.call-update) | async-done | bytes 4194320 | tf_op jit(solution)/shard_map/all_gather | solution.py:47
  94.2 4.6 select_bitcast_fusion
  98.8 16.8 copy.21
  115.6 362.4 %scatter_custom_fusion = f32[16,73728]{0,1:T(8,128)} fusion(s32[65536]{0:T(1024)S(1)} %bitcast.53, f32[65536,16]{1,0:T(8,128)} %copy.21, f32[]{:T(128)} %constant.6.clone.1), kind=kCustom, calls=%fused_computation.4 | custom fusion | flops 1048576 | bytes 4719104 | tf_op jit(solution)/shard_map/scatter-add | solution.py:54
  478.0 20.2 convert_element_type.64
  498.2 16.6 copy.22
  514.8 7.6 fusion.16
  522.4 17.5 copy.23
  539.9 19.2 reshape.130
  559.1 5.8 all-to-all-start
  565.1 1.8 convert_negate_fusion
  566.9 50.9 %all-to-all-done = bf16[32,2,18432]{2,1,0:T(2,128)(2,1)S(1)} async-done(((bf16[32,2,18432]{2,1,0:T(2,128)(2,1)}), bf16[32,2,18432]{2,1,0:T(2,128)(2,1)S(1)}, u32[]{:S(2)}, u32[]{:S(2)}) %all-to-all-start) | async-done | bytes 2359328 | tf_op jit(solution)/shard_map/all_to_all | solution.py:61
  617.8 18.5 reshape.131
  636.3 17.1 copy.31
  653.4 9.2 multiply_reduce_fusion
  662.7 0.8 dynamic-update-slice
  663.4 78.0 %all-reduce.2 = (f32[256]{0:T(256)S(1)}, f32[256]{0:T(256)S(1)}) all-reduce(f32[256]{0:T(256)S(1)} %dynamic-update-slice, f32[256]{0:T(256)S(1)} %dynamic-update-slice.1), channel_id=1, replica_groups=mesh['mem'=8,'band'=32] {'mem','band'}, use_global_device_ids=true, to_apply=%add | all-reduce | flops 512 | bytes 4096
  742.5 1355.0 %while.12 = (s32[]{:T(128)}, f32[]{:T(128)}, f32[]{:T(128)}, f32[255]{0:T(256)S(1)}, f32[255]{0:T(256)S(1)}, /*index=5*/s32[]{:T(128)}) while((s32[]{:T(128)}, f32[]{:T(128)}, f32[]{:T(128)}, f32[255]{0:T(256)S(1)}, f32[255]{0:T(256)S(1)}, /*index=5*/s32[]{:T(128)}) %tuple.26), condition=%wide.region_3.4_spmd, body=%wide.region_2.3_spmd.sunk | while | flops 10 | bytes 197 | solution.py:11
  761.0 0.6 dynamic_slice.10
  766.3 0.6 dynamic_slice.10
  787.6 0.6 dynamic_slice.10
  792.9 0.6 dynamic_slice.10
  814.1 0.6 dynamic_slice.10
  819.5 0.6 dynamic_slice.10
  840.7 0.6 dynamic_slice.10
  862.0 0.6 dynamic_slice.10
  867.3 0.6 dynamic_slice.10
  888.5 0.6 dynamic_slice.10
  893.8 0.6 dynamic_slice.10
  915.1 0.6 dynamic_slice.10
  920.4 0.6 dynamic_slice.10
  941.7 0.6 dynamic_slice.10
  962.9 0.6 dynamic_slice.10
  968.2 0.6 dynamic_slice.10
  989.5 0.6 dynamic_slice.10
  994.8 0.6 dynamic_slice.10
  1016.1 0.6 dynamic_slice.10
  1021.4 0.6 dynamic_slice.10
  1042.6 0.6 dynamic_slice.10
  1063.9 0.6 dynamic_slice.10
  1069.2 0.6 dynamic_slice.10
  1090.5 0.6 dynamic_slice.10
  1095.8 0.6 dynamic_slice.10
  1117.0 0.6 dynamic_slice.10
  1122.3 0.6 dynamic_slice.10
  1143.6 0.6 dynamic_slice.10
  1164.8 0.6 dynamic_slice.10
  1170.2 0.6 dynamic_slice.10
  1191.4 0.6 dynamic_slice.10
  1196.7 0.6 dynamic_slice.10
  1218.0 0.6 dynamic_slice.10
  1223.3 0.6 dynamic_slice.10
  1244.5 0.6 dynamic_slice.10
  1265.8 0.6 dynamic_slice.10
  1271.1 0.6 dynamic_slice.10
  1292.4 0.6 dynamic_slice.10
  2097.5 5.0 copy.26
  (492 shorter events, 278.0 us)
Async XLA Ops:
  7.2 87.0 %all-gather.3.cloned.1.call-start = ((), (), s32[]{:S(2)}) async-start(), calls=%async_computation.1 | async-start | bytes 4325376 | tf_op jit(solution)/shard_map/all_gather | solution.py:47
  52.9 5.8 copy-start.1
  559.1 7.8 copy-start.2
  559.1 58.7 %all-to-all-start = ((bf16[32,2,18432]{2,1,0:T(2,128)(2,1)}), bf16[32,2,18432]{2,1,0:T(2,128)(2,1)S(1)}, u32[]{:S(2)}, u32[]{:S(2)}) async-start(bf16[32,2,18432]{2,1,0:T(2,128)(2,1)} %reshape.130), calls=%async_computation | async-start | bytes 4718592 | tf_op jit(solution)/shard_map/all_to_all | solution.py:61
  636.3 17.1 copy-start
Sparse Core Ops, SparseCore 0:
  11.2 82.9 all-gather.2
where the time goes:
time: 2120 us; the launch traced here: 2110 us
  loops' own time  1060 us (50%)
  local copies, waits for them, and re-layouts  411 us (19%)
  other arithmetic  401 us (19%)
  blocking collectives  120 us (6%)
  waiting for transfers between devices  83.7 us (4%)
    another operation x1, loops' own time, joined(): lax.scan(lambda subtotal, share: (join(subtotal, share), None), head, tail)  1060 us
    scatter-add x1, other arithmetic, on_device(): jnp.zeros((members, cell_count), jnp.float32).at[:, cell_at].add(values)  362 us
    dynamic_slice x510, local copies, waits for them, and re-layouts, joined(): lax.scan(lambda subtotal, share: (join(subtotal, share), None), head, tail)  299 us
    unnamed x1, blocking collectives  78 us
    all_to_all x1, waiting for transfers between devices, on_device(): lax.all_to_all(zonal, 'band', split_axis=3, concat_axis=2, tiled=True)  50.9 us
    unnamed x13, local copies, waits for them, and re-layouts  43.6 us
  transfers between devices with their start and end apart: 2, of which 2 were waited for; matrix products, arithmetic and copies ran while one was open for 1% of the time, Pallas kernels for 0%

commit v1 on v0

v1 whole, which is shorter than its diff:
```python
import math

import jax
import jax.numpy as jnp
from jax import lax
from jax.experimental import pallas as pl
from jax.experimental.pallas import tpu as pltpu
from jax.sharding import PartitionSpec as P

CAP = 128
ROWS = 32
F32 = jnp.float32
BF16 = jnp.bfloat16
VMEM_LIMIT = 56 * 1024 * 1024
LOG2E = 1.4426950408889634


def iota(shape, dim):
    return lax.broadcasted_iota(jnp.int32, shape, dim)


def dot_last(a, b):
    return lax.dot_general(a, b, (((1,), (1,)), ((), ())), preferred_element_type=F32)


def bucket_body(nx, band_ref, cell_ref, weight_ref, pert_ref, out_ref, slot_ref, data_ref):
    bands = out_ref.shape[0]
    members, obs = pert_ref.shape
    earlier = (iota((128, 128), 0) < iota((128, 128), 1)).astype(F32).astype(BF16)
    running = jnp.zeros((bands, 1), F32)
    for part in range(obs // 128):
        at = pl.ds(part * 128, 128)
        target = band_ref[:, at]
        named = (iota((bands, 128), 0) == target).astype(F32)
        before = jnp.dot(named.astype(BF16), earlier, preferred_element_type=F32)
        rank = jnp.sum(named * (before + running), axis=0, keepdims=True)
        slot_ref[:, at] = target * CAP + rank.astype(jnp.int32)
        running = running + jnp.sum(named, axis=1, keepdims=True)
    cell = cell_ref[...]
    row = ((cell.astype(F32) + 0.5) * (1.0 / nx)).astype(jnp.int32)
    col = cell - row * nx
    data_ref[:members, :] = (weight_ref[...] * pert_ref[...].astype(F32)).astype(BF16)
    pick = iota((ROWS - members, obs), 0)
    coords = jnp.where(pick == 0, row, jnp.where(pick == 1, col >> 8, jnp.where(pick == 2, col & 255, 0)))
    data_ref[members:, :] = coords.astype(F32).astype(BF16)

    def fill(dest, carry):
        slots = dest * CAP + iota((CAP, obs), 0)
        move = (slots == slot_ref[...]).astype(F32).astype(BF16)
        out_ref[dest] = dot_last(data_ref[...], move).astype(BF16)
        return carry

    lax.fori_loop(0, bands, fill, 0)


def zonal_body(nx, rows, length_ref, got_ref, out_ref, a_ref, obs_ref):
    srcs = got_ref.shape[0]
    tile = out_ref.shape[0]
    step = pl.program_id(0)
    members = a_ref.shape[0] // rows

    @pl.when(step == 0)
    def _():
        for src in range(srcs):
            at = pl.ds(src * CAP, CAP)
            got = got_ref[src].astype(F32)
            row = got[members : members + 1]
            length = jnp.where(row >= rows // 2, length_ref[1], length_ref[0])
            obs_ref[0:1, at] = got[members + 1 : members + 2] * 256.0 + got[members + 2 : members + 3]
            obs_ref[1:2, at] = LOG2E / length
            obs_ref[2:3, at] = 1.0 - (0.5 * LOG2E) * jnp.log(length)
            here = iota((rows, CAP), 0).astype(F32) == row
            for k in range(members):
                a_ref[k * rows : (k + 1) * rows, at] = jnp.where(here, got[k : k + 1], 0.0).astype(BF16)

    chunk = 512
    total = jnp.zeros((tile, a_ref.shape[0]), F32)
    for part in range(srcs * CAP // chunk):
        at = pl.ds(part * chunk, chunk)
        x = (iota((tile, chunk), 0) + step * tile).astype(F32)
        gap = jnp.abs(x - obs_ref[0:1, at])
        gap = jnp.minimum(gap, nx - gap)
        fx = jnp.exp2(obs_ref[2:3, at] - gap * obs_ref[1:2, at]).astype(BF16)
        total = total + dot_last(fx, a_ref[:, at])
    out_ref[...] = total.astype(BF16)


def final_body(got_ref, fy_ref, control_ref, out_ref, sum_ref, lhs_ref):
    bands, cols, lanes = got_ref.shape
    members, levels, _, ny = out_ref.shape
    rows = lanes // members
    for k in range(members):
        for b0 in range(0, bands, 8):
            lhs_ref[k * cols : (k + 1) * cols, b0 * rows : (b0 + 8) * rows] = jnp.concatenate(
                [got_ref[b, :, k * rows : (k + 1) * rows] for b in range(b0, b0 + 8)], axis=1
            )
    total = jnp.zeros((8, ny), F32)
    for k in range(members):
        for level in range(levels):
            value = jnp.dot(
                lhs_ref[k * cols : (k + 1) * cols, :],
                fy_ref[:, level * ny : (level + 1) * ny],
                preferred_element_type=F32,
            )
            value = value + control_ref[k, level].astype(F32)
            out_ref[k, level] = value
            total = total + jnp.sum((value * value).reshape(cols // 8, 8, ny), axis=0)

    @pl.when(pl.program_id(0) == 0)
    def _():
        sum_ref[...] = total

    @pl.when(pl.program_id(0) > 0)
    def _():
        sum_ref[...] = sum_ref[...] + total


def on_device(control, member_pert, obs_weight, obs_band, obs_cell, length_x, length_y):
    members, levels, x_block, ny = control.shape
    bands = lax.axis_size("band")
    groups = lax.axis_size("mem")
    ny_loc = ny // bands
    nx = x_block * bands
    obs = obs_cell.shape[0]
    rows = levels * ny_loc
    params = pltpu.CompilerParams(vmem_limit_bytes=VMEM_LIMIT)

    packed = pl.pallas_call(
        lambda *refs: bucket_body(nx, *refs),
        out_shape=jax.ShapeDtypeStruct((bands, ROWS, CAP), BF16),
        scratch_shapes=[pltpu.VMEM((1, obs), jnp.int32), pltpu.VMEM((ROWS, obs), BF16)],
        compiler_params=params,
        name="bucket",
    )(obs_band.reshape(1, obs), obs_cell.reshape(1, obs), obs_weight.reshape(1, obs), member_pert)
    got = lax.all_to_all(packed, "band", 0, 0, tiled=True)

    tile = 256
    zonal = pl.pallas_call(
        lambda *refs: zonal_body(nx, rows, *refs),
        grid=(nx // tile,),
        in_specs=[
            pl.BlockSpec(memory_space=pltpu.SMEM),
            pl.BlockSpec((bands, ROWS, CAP), lambda i: (0, 0, 0)),
        ],
        out_specs=pl.BlockSpec((tile, members * rows), lambda i: (i, 0)),
        out_shape=jax.ShapeDtypeStruct((nx, members * rows), BF16),
        scratch_shapes=[pltpu.VMEM((members * rows, bands * CAP), BF16), pltpu.VMEM((8, bands * CAP), F32)],
        compiler_params=params,
        name="zonal",
    )(length_x, got)
    turned = lax.all_to_all(zonal.reshape(bands, x_block, members * rows), "band", 0, 0, tiled=True)

    at = jnp.arange(bands * rows, dtype=jnp.int32)
    at_level, at_y = (at % rows) // ny_loc, at // rows * ny_loc + at % ny_loc
    to = jnp.arange(levels * ny, dtype=jnp.int32)
    to_level, to_y = to // ny, to % ny
    gap = jnp.abs(at_y[:, None] - to_y[None, :]).astype(F32)
    length = length_y[to_level][None, :]
    filter_y = jnp.where(
        at_level[:, None] == to_level[None, :], 2.0 / jnp.sqrt(length) * jnp.exp(-gap / length), 0.0
    ).astype(BF16)

    part = 8
    gradient, squares = pl.pallas_call(
        final_body,
        grid=(members // part,),
        in_specs=[
            pl.BlockSpec((bands, x_block, part * rows), lambda i: (0, 0, i)),
            pl.BlockSpec((bands * rows, levels * ny), lambda i: (0, 0)),
            pl.BlockSpec((part, levels, x_block, ny), lambda i: (i, 0, 0, 0)),
        ],
        out_specs=[
            pl.BlockSpec((part, levels, x_block, ny), lambda i: (i, 0, 0, 0)),
            pl.BlockSpec((8, ny), lambda i: (0, 0)),
        ],
        out_shape=[
            jax.ShapeDtypeStruct((members, levels, x_block, ny), F32),
            jax.ShapeDtypeStruct((8, ny), F32),
        ],
        scratch_shapes=[pltpu.VMEM((part * x_block, bands * rows), BF16)],
        compiler_params=params,
        name="final",
    )(turned, filter_y, control)

    partial_value = jnp.broadcast_to(jnp.sum(squares), (groups * bands, 1, 128))
    partials = lax.all_to_all(partial_value, ("mem", "band"), 0, 0, tiled=True)
    gradient_dot = jnp.sum(partials[:, 0, 0]) * (1.0 / (members * groups * levels * ny * nx))
    return (gradient, gradient_dot)


def solution(mesh):
    return jax.shard_map(
        on_device,
        mesh=mesh,
        in_specs=(
            P("mem", None, "band", None),
            P("mem", "band"),
            P("band"),
            P("band", None),
            P("band"),
            P(),
            P(),
        ),
        out_specs=(P("mem", None, "band", None), P()),
        check_vma=False,
    )
```

time: 2120 us -> 159 us (0.07)
  loops' own time: 1060 us -> 0 us
  local copies, waits for them, and re-layouts: 411 us -> 2.76 us
  other arithmetic: 401 us -> 11.7 us
  blocking collectives: 120 us -> 45.4 us
  Pallas kernels: 0 us -> 45.1 us
  waiting for transfers between devices: 83.7 us -> 44.6 us
    another operation x1 -> x0, loops' own time: 1060 us -> none  [joined(): lax.scan(lambda subtotal, share: (join(subtotal, share), None), head, tail)]
    scatter-add x1 -> x0, other arithmetic: 362 us -> none  [on_device(): jnp.zeros((members, cell_count), jnp.float32).at[:, cell_at].add(values)]
    dynamic_slice x510 -> x0, local copies, waits for them, and re-layouts: 299 us -> none  [joined(): lax.scan(lambda subtotal, share: (join(subtotal, share), None), head, tail)]
    unnamed x1 -> x0, blocking collectives: 78 us -> none
    all_to_all x0 -> x2, blocking collectives: none -> 45.4 us  [the longest x1 23.5 us: on_device(): partials = lax.all_to_all(partial_value, ('mem', 'band'), 0, 0, tiled=True)]
    pallas_call x0 -> x3, Pallas kernels: none -> 45.1 us  [the longest x1 18 us: on_device(): pl.pallas_call(final_body, grid=(members // part,), in_specs=[pl.BlockSpe...]
    all_gather x1 -> x0, blocking collectives: 42.4 us -> none  [on_device(): lax.all_gather(placed, 'band', axis=1, tiled=True)]
    unnamed x13 -> x4, local copies, waits for them, and re-layouts: 43.6 us -> 1.45 us
  transfers between devices with their start and end apart: 2 -> 1, of which waited for: 2 -> 1; matrix products, arithmetic and copies ran while one was open for 1% -> 6% of each run, Pallas kernels for 0% -> 0%
where the time goes in v1:
time: 159 us; the launch traced here: 158 us
  blocking collectives  45.4 us (29%)
  Pallas kernels  45.1 us (28%)
  waiting for transfers between devices  44.6 us (28%)
  other arithmetic  11.7 us (7%)
  starting transfers between devices  6.3 us (4%)
  local copies, waits for them, and re-layouts  2.76 us (2%)
  between operations  2.47 us (2%)
    all_to_all x1, waiting for transfers between devices, on_device(): lax.all_to_all(zonal.reshape(bands, x_block, members * rows), 'band', 0,...  44.6 us
    all_to_all x1, blocking collectives, on_device(): partials = lax.all_to_all(partial_value, ('mem', 'band'), 0, 0, tiled=True)  23.5 us
    all_to_all x1, blocking collectives, on_device(): got = lax.all_to_all(packed, 'band', 0, 0, tiled=True)  21.8 us
    pallas_call x1, Pallas kernels, on_device(): pl.pallas_call(final_body, grid=(members // part,), in_specs=[pl.BlockSpe...  18 us
    pallas_call x1, Pallas kernels, on_device(): pl.pallas_call(lambda *refs: zonal_body(nx, rows, *refs), grid=(nx // til...  16 us
    pallas_call x1, Pallas kernels, on_device(): pl.pallas_call(lambda *refs: bucket_body(nx, *refs), out_shape=jax.ShapeD...  11.1 us
    convert_element_type x1, other arithmetic, on_device(): filter_y = jnp.where(at_level[:, None] == to_level[None, :], 2.0 / jnp.sq...  8.07 us
    all_to_all x1, starting transfers between devices, on_device(): lax.all_to_all(zonal.reshape(bands, x_block, members * rows), 'band', 0,...  6.3 us
  transfers between devices with their start and end apart: 1, of which 1 were waited for; matrix products, arithmetic and copies ran while one was open for 6% of the time, Pallas kernels for 0%

profile of v1, /device:TPU:1, one launch (start us, length us, event | category | flops | bytes accessed | tf_op | source)
XLA Modules:
  0.0 158.3 jit_solution(5878327047461378218)
XLA Ops:
  0.6 0.0 copy-start.1
  0.6 11.1 %bucket.1 = bf16[32,32,128]{2,1,0:T(8,128)(2,1)} custom-call(s32[1,2048]{1,0:T(1,128)} %bitcast.7, s32[1,2048]{1,0:T(1,128)} %bitcast.8, f32[1,2048]{1,0:T(1,128)} %bitcast.9, bf16[16,2048]{1,0:T(8,128)(2,1)} %refs_3_.1), custom_call_target="tpu_custom_call" | custom-call | tf_op jit(solution)/shard_map/bucket/pallas_call | solution.py:128
  11.7 21.8 %all_to_all.15.refs_1_ = bf16[32,32,128]{2,1,0:T(8,128)(2,1)} all-to-all(bf16[32,32,128]{2,1,0:T(8,128)(2,1)} %bucket.1), channel_id=1, replica_groups=mesh['mem'=8,'band'=32] {'band'}, dimensions={0} | all-to-all | bytes 524288 | tf_op jit(solution)/shard_map/all_to_all | solution.py:135
  33.5 16.0 %zonal.1 = bf16[1536,768]{1,0:T(8,128)(2,1)} custom-call(f32[2]{0:T(128)} %refs_0_.1, bf16[32,32,128]{2,1,0:T(8,128)(2,1)} %all_to_all.15.refs_1_), custom_call_target="tpu_custom_call" | custom-call | tf_op jit(solution)/shard_map/zonal/pallas_call | solution.py:138
  49.6 6.3 %all-to-all-start.1 = ((bf16[32,48,768]{2,1,0:T(8,128)(2,1)}), bf16[32,48,768]{2,1,0:T(8,128)(2,1)S(1)}, u32[]{:S(2)}, u32[]{:S(2)}) async-start(bf16[32,48,768]{2,1,0:T(8,128)(2,1)} %bitcast.6), calls=%async_computation.1 | async-start | bytes 4718592 | tf_op jit(solution)/shard_map/all_to_all | solution.py:151
  55.9 0.0 copy-done.1
  55.9 0.6 fusion.18
  56.5 1.4 fusion.17
  57.9 8.1 %select_convert_fusion.fy_ref = bf16[1536,1536]{1,0:T(8,128)(2,1)} fusion(f32[1536]{0:T(1024)S(1)} %fusion.17, s32[1536]{0:T(1024)S(1)} %get-tuple-element.8, s32[1536]{0:T(1024)S(1)} %get-tuple-element.11, f32[1536]{0:T(1024)S(1)} %rsqrt_multiply_fusion, s32[1536]{0:T(1024)S(1)} %get-tuple-element.9, s32[1536]{0:T(1024)S(1)} %get-tuple-element.10), kind=kLoop, calls=%fused_computation | loop fusion | flops 21233664 | bytes 4755456 | tf_op jit(solution)/shard_map/convert_element_type | solution.py:161
  66.0 44.6 %all-to-all-done.1.got_ref = bf16[32,48,768]{2,1,0:T(8,128)(2,1)S(1)} async-done(((bf16[32,48,768]{2,1,0:T(8,128)(2,1)}), bf16[32,48,768]{2,1,0:T(8,128)(2,1)S(1)}, u32[]{:S(2)}, u32[]{:S(2)}) %all-to-all-start.1) | async-done | bytes 2359328 | tf_op jit(solution)/shard_map/all_to_all | solution.py:151
  110.6 0.0 copy-start
  110.6 1.4 copy-done
  112.0 18.0 %final.1 = (f32[16,2,48,768]{3,2,1,0:T(8,128)}, f32[8,768]{1,0:T(8,128)}) custom-call(bf16[32,48,768]{2,1,0:T(8,128)(2,1)} %copy-done, bf16[1536,1536]{1,0:T(8,128)(2,1)} %select_convert_fusion.fy_ref, bf16[16,2,48,768]{3,2,1,0:T(8,128)(2,1)} %control_ref.1), custom_call_target="tpu_custom_call" | custom-call | tf_op jit(solution)/shard_map/final/pallas_call | solution.py:164
  130.1 1.3 reduce_sum.18
  131.4 0.7 broadcast_in_dim.6
  132.2 23.5 %all_to_all.16 = f32[256,1,128]{2,1,0:T(1,128)S(1)} all-to-all(f32[256,1,128]{2,1,0:T(1,128)S(1)} %broadcast_in_dim.6), channel_id=1, replica_groups=mesh['mem'=8,'band'=32] {'mem','band'}, dimensions={0} | all-to-all | bytes 262144 | tf_op jit(solution)/shard_map/all_to_all | solution.py:186
  155.7 0.9 slice_reduce_fusion
  (3 shorter events, 0.0 us)
Async XLA Ops:
  0.6 55.2 %copy-start.1 = (f32[2]{0:T(128)S(1)}, f32[2]{0:T(128)}, u32[]{:S(2)}) copy-start(f32[2]{0:T(128)} %param.13) | copy-start | bytes 28
  49.6 61.0 %all-to-all-start.1 = ((bf16[32,48,768]{2,1,0:T(8,128)(2,1)}), bf16[32,48,768]{2,1,0:T(8,128)(2,1)S(1)}, u32[]{:S(2)}, u32[]{:S(2)}) async-start(bf16[32,48,768]{2,1,0:T(8,128)(2,1)} %bitcast.6), calls=%async_computation.1 | async-start | bytes 4718592 | tf_op jit(solution)/shard_map/all_to_all | solution.py:151
  110.6 1.4 copy-start

commit v2 on v0

v2 whole, which is shorter than its diff:
```python
import jax
import jax.numpy as jnp
from jax import lax
from jax.experimental import pallas as pl
from jax.experimental.pallas import tpu as pltpu
from jax.sharding import PartitionSpec as P

CAP = 128
HALF = 64
KEPT = 24
F32 = jnp.float32
BF16 = jnp.bfloat16
LOG2E = 1.4426950408889634
PARAMS = pltpu.CompilerParams(vmem_limit_bytes=56 * 1024 * 1024)
SMEM = pl.BlockSpec(memory_space=pltpu.SMEM)


def iota(shape, dim):
    return lax.broadcasted_iota(jnp.int32, shape, dim)


def flag(mask):
    return mask.astype(F32).astype(BF16)


def dot_last(a, b):
    return lax.dot_general(a, b, (((1,), (1,)), ((), ())), preferred_element_type=F32)


def rates(length):
    return LOG2E / length, 1.0 - (0.5 * LOG2E) * jnp.log(length)


def bucket_body(
    nx, rows, x_block, turn_ref, band_ref, cell_ref, weight_ref, pert_ref, out_ref, slot_ref, data_ref, masked_ref
):
    ends = out_ref.shape[0]
    members, obs = pert_ref.shape
    turn = turn_ref[0]
    earlier = flag(iota((128, 128), 0) < iota((128, 128), 1))
    cell = cell_ref[...]
    band = band_ref[...]
    row = ((cell.astype(F32) + 0.5) * (1.0 / nx)).astype(jnp.int32)
    col = cell - row * nx
    block = ((col.astype(F32) + 0.5) * (1.0 / x_block)).astype(jnp.int32)
    level = (row >= rows // 2).astype(jnp.int32)
    within = col - block * x_block
    data_ref[:members, :] = (weight_ref[...] * pert_ref[...].astype(F32)).astype(BF16)
    pick = iota((data_ref.shape[0] - members, obs), 0)
    coords = jnp.where(
        pick == 0, band, jnp.where(pick == 1, row, jnp.where(pick == 2, within, jnp.where(pick == 3, block, 0)))
    )
    data_ref[members:, :] = coords.astype(F32).astype(BF16)

    running = jnp.zeros((3 * ends, 1), F32)
    for part in range(obs // 128):
        at = slice(part * 128, (part + 1) * 128)
        key = iota((3 * ends, 128), 0)
        named = ((key == block[:, at] + ends * level[:, at]) | (key == band[:, at] + 2 * ends)).astype(F32)
        before = named * (jnp.dot(named.astype(BF16), earlier, preferred_element_type=F32) + running)
        rank = jnp.sum(before[: 2 * ends], axis=0, keepdims=True).astype(jnp.int32) - turn * HALF
        fits = (rank >= 0) & (rank < HALF)
        slot_ref[0:1, at] = jnp.where(fits, rank + HALF * level[:, at], -1)
        slot_ref[1:2, at] = jnp.sum(before[2 * ends :], axis=0, keepdims=True).astype(jnp.int32)
        running = running + jnp.sum(named, axis=1, keepdims=True)
    most = jnp.max(running[: 2 * ends], axis=0, keepdims=True).astype(jnp.int32)
    rounds = ((most + (HALF - 1)) >> 6).astype(F32)

    size = data_ref.shape[0]
    for side, dest in ((0, block), (1, band)):
        move = flag(iota((CAP, obs), 0) == slot_ref[side : side + 1, :])
        for end in range(ends):
            masked_ref[end * size : (end + 1) * size, :] = data_ref[...] * flag(dest == end)
        for end in range(0, ends, 8):
            packed = dot_last(masked_ref[end * size : (end + 8) * size, :], move).reshape(8, size, CAP)[:, :KEPT]
            if side == 0:
                packed = jnp.where(iota(packed.shape, 1) == members + 4, rounds[None], packed)
            out_ref[end : end + 8, :, side * CAP : (side + 1) * CAP] = packed.astype(BF16)


def states_body(rows, x_block, length_ref, got_ref, out_ref, a_ref, obs_ref):
    srcs = got_ref.shape[0]
    members = a_ref.shape[0] // rows
    for src in range(srcs):
        at = pl.ds(src * CAP, CAP)
        got = got_ref[src].astype(F32)
        row = got[members + 1 : members + 2]
        obs_ref[0:3, at] = got[members + 1 : members + 4]
        here = iota((rows, CAP), 0).astype(F32) == row
        for k in range(members):
            a_ref[k * rows : (k + 1) * rows, at] = jnp.where(here, got[k : k + 1], 0.0).astype(BF16)
    length = jnp.where(obs_ref[0:1, :] >= rows // 2, length_ref[1], length_ref[0])
    rate, scale = rates(length)
    within = obs_ref[1:2, :]
    place = iota((2 * srcs, srcs * CAP), 0)
    right = (place & 1) == 1
    ahead = (place >> 1) - obs_ref[2:3, :].astype(jnp.int32)
    steps = jnp.where(right, -ahead, ahead) & (srcs - 1)
    gap = (steps * x_block).astype(F32) + jnp.where(right, within - (x_block - 1.0), -within)
    apart = (steps >= 1) & (steps < srcs // 2)
    edge = jnp.where(apart, jnp.exp2(scale - jnp.maximum(gap, 0.0) * rate), 0.0).astype(BF16)
    value = dot_last(edge, a_ref[...]).astype(BF16)
    for block in range(srcs):
        out_ref[block] = value[2 * block : 2 * block + 2]


def decays(length, shape):
    rate = LOG2E / jnp.full(shape, length, F32)
    x = iota(shape, 0).astype(F32)
    return jnp.exp2(-x * rate), jnp.exp2((x - (shape[0] - 1.0)) * rate)


def near_body(
    ny_loc, nx, length_x_ref, length_y_ref, own_ref, far_ref, base_ref, out_ref, moments_ref, obs_ref, a_ref
):
    srcs = own_ref.shape[0]
    members, _, cols, ny = out_ref.shape
    level = pl.program_id(0)
    lanes = srcs * HALF
    first = iota((KEPT, CAP), 1) < HALF
    for which, ref in enumerate((own_ref, far_ref)):
        for src in range(0, srcs, 2):
            one, two = ref[src].astype(F32), ref[src + 1].astype(F32)
            low = jnp.where(first, one, pltpu.roll(two, HALF, 1))
            high = jnp.where(first, pltpu.roll(one, HALF, 1), two)
            at = which * lanes + src * HALF
            obs_ref[:, at : at + CAP] = jnp.where(level == 0, low, high)

    def constants(ref):
        return rates(jnp.full((1, CAP), ref[level], F32))

    def wide(value, shape):
        return jnp.broadcast_to(value[:, :1], shape)

    (rate_x, scale_x), (rate_y, scale_y) = constants(length_x_ref), constants(length_y_ref)
    chunk = 512
    total = jnp.zeros((members * cols, ny), F32)
    for part in range(2 * lanes // chunk):
        at = slice(part * chunk, (part + 1) * chunk)
        gap = jnp.abs(iota((cols, chunk), 0).astype(F32) - obs_ref[members + 2 : members + 3, at])
        if part * chunk >= lanes:
            gap = nx // 2 - gap
        filter_x = jnp.exp2(wide(scale_x, (1, chunk)) - gap * wide(rate_x, (1, chunk)))
        for k in range(members):
            a_ref[k * cols : (k + 1) * cols, at] = (filter_x * obs_ref[k : k + 1, at]).astype(BF16)
        row = obs_ref[members + 1 : members + 2, at] - (level * ny_loc).astype(F32)
        y = obs_ref[members : members + 1, at] * ny_loc + jnp.maximum(row, 0.0)
        gap = jnp.abs(iota((ny, chunk), 0).astype(F32) - y)
        filter_y = jnp.exp2(wide(scale_y, (1, chunk)) - gap * wide(rate_y, (1, chunk))).astype(BF16)
        total = total + dot_last(a_ref[:, at], filter_y)
    left, right = decays(length_x_ref[level], (cols, ny))
    for k in range(members):
        value = base_ref[k, 0].astype(F32) + total[k * cols : (k + 1) * cols]
        out_ref[k, 0] = value
        for which, factor in enumerate((left, right, value)):
            moments_ref[which, 0, k : k + 1] = jnp.sum(value * factor, axis=0, keepdims=True)


def edge_body(cols, length_x_ref, got_ref, fy_ref, moments_ref, out_ref, sum_ref, lhs_ref):
    bands, _, lanes = got_ref.shape
    _, levels, members, ny = out_ref.shape
    rows = lanes // members
    got = [got_ref[b].astype(F32) for b in range(bands)]
    for k in range(members):
        piece = jnp.concatenate([got[b][:, k * rows : (k + 1) * rows] for b in range(bands)], axis=1)
        lhs_ref[k : k + 1, :] = piece[0:1]
        lhs_ref[members + k : members + k + 1, :] = piece[1:2]
    edge = jnp.dot(lhs_ref[...].astype(BF16), fy_ref[...], preferred_element_type=F32)
    total = jnp.zeros((members, ny), F32)
    for level in range(levels):
        at = slice(level * ny, (level + 1) * ny)
        one, two = edge[:members, at], edge[members:, at]
        out_ref[0, level], out_ref[1, level] = one, two
        left, right = decays(length_x_ref[level], (cols, 128))

        def over_columns(value):
            return jnp.sum(value, axis=0, keepdims=True)[:, :1]

        total = total + moments_ref[2, level]
        total = total + one * (2.0 * moments_ref[0, level] + one * over_columns(left * left))
        total = total + two * (2.0 * moments_ref[1, level] + two * over_columns(right * right))
        total = total + one * two * (2.0 * over_columns(left * right))
    sum_ref[...] = jnp.full(sum_ref.shape, jnp.sum(total), F32)


def final_body(length_x_ref, edge_ref, near_ref, out_ref):
    part, levels, cols, ny = out_ref.shape
    for level in range(levels):
        left, right = decays(length_x_ref[level], (cols, ny))
        for k in range(part):
            one, two = edge_ref[0, level, k : k + 1], edge_ref[1, level, k : k + 1]
            out_ref[k, level] = near_ref[k, level] + left * one + right * two


def on_device(control, member_pert, obs_weight, obs_band, obs_cell, length_x, length_y):
    members, levels, x_block, ny = control.shape
    bands = lax.axis_size("band")
    groups = lax.axis_size("mem")
    ny_loc = ny // bands
    nx = x_block * bands
    obs = obs_cell.shape[0]
    rows = levels * ny_loc
    size = 32

    def route(turn, beside):
        packed = pl.pallas_call(
            lambda *refs: bucket_body(nx, rows, x_block, *refs),
            in_specs=[SMEM] + [pl.BlockSpec(memory_space=pltpu.VMEM)] * 4,
            out_shape=jax.ShapeDtypeStruct((bands, KEPT, 2 * CAP), BF16),
            scratch_shapes=[
                pltpu.VMEM((8, obs), jnp.int32),
                pltpu.VMEM((size, obs), BF16),
                pltpu.VMEM((bands * size, obs), BF16),
            ],
            compiler_params=PARAMS,
            name="bucket",
        )(turn, obs_band.reshape(1, obs), obs_cell.reshape(1, obs), obs_weight.reshape(1, obs), member_pert)
        got = lax.all_to_all(packed, "band", 0, 0, tiled=True)
        if beside is not None:
            got, beside = lax.optimization_barrier((got, beside))
        swap = [(i, (i + bands // 2) % bands) for i in range(bands)]
        return got, lax.ppermute(got[:, :, :CAP], "band", swap), beside

    def near_field(got, opposite, base):
        by_level = pl.BlockSpec((members, 1, x_block, ny), lambda i: (0, i, 0, 0))
        slots = 2 * bands * HALF
        return pl.pallas_call(
            lambda *refs: near_body(ny_loc, nx, *refs),
            grid=(levels,),
            in_specs=[
                SMEM,
                SMEM,
                pl.BlockSpec((bands, KEPT, CAP), lambda i: (0, 0, 0)),
                pl.BlockSpec((bands, KEPT, CAP), lambda i: (0, 0, 0)),
                by_level,
            ],
            out_specs=[by_level, pl.BlockSpec((3, 1, members, ny), lambda i: (0, i, 0, 0))],
            out_shape=[
                jax.ShapeDtypeStruct((members, levels, x_block, ny), F32),
                jax.ShapeDtypeStruct((3, levels, members, ny), F32),
            ],
            scratch_shapes=[pltpu.VMEM((KEPT, slots), F32), pltpu.VMEM((members * x_block, slots), BF16)],
            compiler_params=PARAMS,
            cost_estimate=pl.CostEstimate(
                flops=2 * levels * members * x_block * slots * ny, bytes_accessed=8_000_000, transcendentals=7_000_000
            ),
            name="near",
        )(length_x, length_y, got, opposite, base)

    at = jnp.arange(bands * rows, dtype=jnp.int32)
    at_level, at_y = (at % rows) // ny_loc, at // rows * ny_loc + at % ny_loc
    to = jnp.arange(levels * ny, dtype=jnp.int32)
    to_level, to_y = to // ny, to % ny
    gap = jnp.abs(at_y[:, None] - to_y[None, :]).astype(F32)
    length = length_y[to_level][None, :]
    filter_y = jnp.where(
        at_level[:, None] == to_level[None, :], 2.0 / jnp.sqrt(length) * jnp.exp(-gap / length), 0.0
    ).astype(BF16)

    got, opposite, filter_y = route(jnp.zeros((1,), jnp.int32), filter_y)
    states = pl.pallas_call(
        lambda *refs: states_body(rows, x_block, *refs),
        grid=(1,),
        in_specs=[SMEM, pl.BlockSpec((bands, KEPT, CAP), lambda i: (0, 0, 1))],
        out_specs=pl.BlockSpec((bands, 2, members * rows), lambda i: (0, 0, 0)),
        out_shape=jax.ShapeDtypeStruct((bands, 2, members * rows), BF16),
        scratch_shapes=[pltpu.VMEM((members * rows, bands * CAP), BF16), pltpu.VMEM((8, bands * CAP), F32)],
        compiler_params=PARAMS,
        name="states",
    )(length_x, got)
    edges = lax.all_to_all(states, "band", 0, 0, tiled=True)

    near, moments = near_field(got, opposite, control)
    rounds = jnp.max(got[:, members + 4, 0].astype(F32)).astype(jnp.int32)

    def again(carry):
        turn, near, _ = carry
        more, more_opposite, _ = route(turn.reshape(1), None)
        return (turn + 1, *near_field(more, more_opposite, near))

    _, near, moments = lax.while_loop(lambda carry: carry[0] < rounds, again, (jnp.int32(1), near, moments))

    edge, partial_value = pl.pallas_call(
        lambda *refs: edge_body(x_block, *refs),
        in_specs=[SMEM] + [pl.BlockSpec(memory_space=pltpu.VMEM)] * 3,
        out_shape=[
            jax.ShapeDtypeStruct((2, levels, members, ny), F32),
            jax.ShapeDtypeStruct((groups * bands, 128), F32),
        ],
        scratch_shapes=[pltpu.VMEM((2 * members, bands * rows), F32)],
        compiler_params=PARAMS,
        name="edge",
    )(length_x, edges, filter_y, moments)
    partials = lax.all_to_all(partial_value, ("mem", "band"), 0, 0, tiled=True)

    part = 8
    by_member = pl.BlockSpec((part, levels, x_block, ny), lambda i: (i, 0, 0, 0))
    gradient = pl.pallas_call(
        final_body,
        grid=(members // part,),
        in_specs=[SMEM, pl.BlockSpec((2, levels, part, ny), lambda i: (0, 0, i, 0)), by_member],
        out_specs=by_member,
        out_shape=jax.ShapeDtypeStruct((members, levels, x_block, ny), F32),
        compiler_params=PARAMS,
        cost_estimate=pl.CostEstimate(flops=20_000_000, bytes_accessed=10_000_000, transcendentals=0),
        name="final",
    )(length_x, edge, near)
    gradient_dot = jnp.sum(partials[:, 0]) * (1.0 / (members * groups * levels * ny * nx))
    return (gradient, gradient_dot)


def solution(mesh):
    return jax.shard_map(
        on_device,
        mesh=mesh,
        in_specs=(
            P("mem", None, "band", None),
            P("mem", "band"),
            P("band"),
            P("band", None),
            P("band"),
            P(),
            P(),
        ),
        out_specs=(P("mem", None, "band", None), P()),
        check_vma=False,
    )
```

time: 2120 us -> 98 us (0.05)
  loops' own time: 1060 us -> 0.01 us
  local copies, waits for them, and re-layouts: 411 us -> 2.66 us
  other arithmetic: 401 us -> 10.7 us
  blocking collectives: 120 us -> 0 us
  waiting for transfers between devices: 83.7 us -> 12.3 us
  Pallas kernels: 0 us -> 33.1 us
  starting transfers between devices: 5.79 us -> 35.7 us
    another operation x1, loops' own time: 1060 us -> 0.01 us  [on_device(): lax.while_loop(lambda carry: carry[0] < rounds, again, (jnp.int32(1), nea...]
    scatter-add x1 -> x0, other arithmetic: 362 us -> none  [on_device(): jnp.zeros((members, cell_count), jnp.float32).at[:, cell_at].add(values)]
    dynamic_slice x510 -> x0, local copies, waits for them, and re-layouts: 299 us -> none  [joined(): lax.scan(lambda subtotal, share: (join(subtotal, share), None), head, tail)]
    unnamed x1 -> x0, blocking collectives: 78 us -> none
    all_gather x1 -> x0, blocking collectives: 42.4 us -> none  [on_device(): lax.all_gather(placed, 'band', axis=1, tiled=True)]
    unnamed x13 -> x18, local copies, waits for them, and re-layouts: 43.6 us -> 1.3 us
    all_to_all x1 -> x3, waiting for transfers between devices: 50.9 us -> 12.3 us  [the longest x1 8.76 us: on_device(): partials = lax.all_to_all(partial_value, ('mem', 'band'), 0, 0, tiled=True)]
    convert_element_type x2 -> x0, local copies, waits for them, and re-layouts: 34.1 us -> none  [the longest x1 17.5 us: on_device(): zonal = jnp.einsum('klyx,lxw->klyw', grid_sum, filter_x, preferred_elemen...]
  transfers between devices with their start and end apart: 2 -> 4, of which waited for: 2 -> 2; matrix products, arithmetic and copies ran while one was open for 1% -> 9% of each run, Pallas kernels for 0% -> 25%
where the time goes in v2:
time: 98 us; the launch traced here: 97.6 us
  starting transfers between devices  35.7 us (36%)
  Pallas kernels  33.1 us (34%)
  waiting for transfers between devices  12.3 us (13%)
  other arithmetic  10.7 us (11%)
  between operations  3.14 us (3%)
  local copies, waits for them, and re-layouts  2.66 us (3%)
    pallas_call x1, Pallas kernels, near_field(): pl.pallas_call(lambda *refs: near_body(ny_loc, nx, *refs), grid=(levels,)...  15.5 us
    all_to_all x1, starting transfers between devices, on_device(): partials = lax.all_to_all(partial_value, ('mem', 'band'), 0, 0, tiled=True)  14.7 us
    all_to_all x1, starting transfers between devices, route(): got = lax.all_to_all(packed, 'band', 0, 0, tiled=True)  12 us
    all_to_all x1, waiting for transfers between devices, on_device(): partials = lax.all_to_all(partial_value, ('mem', 'band'), 0, 0, tiled=True)  8.76 us
    convert_element_type x1, other arithmetic, on_device(): filter_y = jnp.where(at_level[:, None] == to_level[None, :], 2.0 / jnp.sq...  8.07 us
    all_to_all x1, starting transfers between devices, on_device(): edges = lax.all_to_all(states, 'band', 0, 0, tiled=True)  7.34 us
    pallas_call x1, Pallas kernels, on_device(): pl.pallas_call(lambda *refs: edge_body(x_block, *refs), in_specs=[SMEM] +...  4.54 us
    pallas_call x1, Pallas kernels, route(): pl.pallas_call(lambda *refs: bucket_body(nx, rows, x_block, *refs), in_sp...  4.41 us
  transfers between devices with their start and end apart: 4, of which 2 were waited for; matrix products, arithmetic and copies ran while one was open for 9% of the time, Pallas kernels for 25%

profile of v2, /device:TPU:1, one launch (start us, length us, event | category | flops | bytes accessed | tf_op | source)
XLA Modules:
  0.0 97.6 jit_solution(17774440919606784154)
XLA Ops:
  0.6 0.0 copy-start.8
  0.6 0.0 copy-start.7
  0.7 1.3 %fusion.18 = (f32[1]{0:T(128)}, f32[1]{0:T(128)}) fusion(f32[2]{0:T(128)} %refs_1_.1), kind=kLoop, calls=%fused_computation.41 | loop fusion | bytes 16 | tf_op jit(solution)/shard_map/gather | solution.py:255
  2.0 1.3 %fusion.17 = f32[1536]{0:T(1024)S(1)} fusion(f32[]{:T(128)} %bitcast.8, f32[]{:T(128)} %bitcast.7), kind=kLoop, calls=%fused_computation.40 | loop fusion | flops 19968 | bytes 6152 | tf_op jit(solution)/shard_map/gather | solution.py:255
  3.4 4.4 %bucket.2 = bf16[32,24,256]{2,1,0:T(8,128)(2,1)} custom-call(s32[1]{0:T(128)} %constant.50.clone.1.refs_0_, s32[1,2048]{1,0:T(1,128)} %bitcast.22, s32[1,2048]{1,0:T(1,128)} %bitcast.24, f32[1,2048]{1,0:T(1,128)} %bitcast.26, bf16[16,2048]{1,0:T(8,128)(2,1)} %refs_4_.2), custom_call_target="tpu_custom_call" | custom-call | tf_op jit(solution)/shard_map/bucket/pallas_call | solution.py:206
  7.8 12.0 %all-to-all-start.1 = ((bf16[32,24,256]{2,1,0:T(8,128)(2,1)}), bf16[32,24,256]{2,1,0:T(8,128)(2,1)S(1)}, u32[]{:S(2)}, u32[]{:S(2)}) async-start(bf16[32,24,256]{2,1,0:T(8,128)(2,1)} %bucket.2), calls=%async_computation.1 | async-start | bytes 786432 | tf_op jit(solution)/shard_map/all_to_all | solution.py:218
  19.8 8.1 %select_convert_fusion.refs_2_ = bf16[1536,1536]{1,0:T(8,128)(2,1)} fusion(f32[1536]{0:T(1024)S(1)} %fusion.17, s32[1536]{0:T(1024)S(1)} %get-tuple-element.93, s32[1536]{0:T(1024)S(1)} %get-tuple-element.96, f32[1536]{0:T(1024)S(1)} %rsqrt_multiply_fusion, s32[1536]{0:T(1024)S(1)} %get-tuple-element.94, s32[1536]{0:T(1024)S(1)} %get-tuple-element.95), kind=kLoop, calls=%fused_computation | loop fusion | flops 21233664 | bytes 4755456 | tf_op jit(solution)/shard_map/convert_element_type | solution.py:258
  27.9 3.6 %all-to-all-done.1.refs_1_.refs_2_ = bf16[32,24,256]{2,1,0:T(8,128)(2,1)S(1)} async-done(((bf16[32,24,256]{2,1,0:T(8,128)(2,1)}), bf16[32,24,256]{2,1,0:T(8,128)(2,1)S(1)}, u32[]{:S(2)}, u32[]{:S(2)}) %all-to-all-start.1) | async-done | bytes 393248 | tf_op jit(solution)/shard_map/all_to_all | solution.py:218
  31.5 0.0 copy-start.1
  31.5 1.7 %collective-permute-start.1 = (bf16[32,24,128]{2,1,0:T(8,128)(2,1)S(1)}, bf16[32,24,128]{2,1,0:T(8,128)(2,1)S(1)}, u32[]{:S(2)}, u32[]{:S(2)}) collective-permute-start(bf16[32,24,128]{2,1,0:T(8,128)(2,1)S(1)} %slice.12), channel_id=1, source_target_pairs={{0,16},{1,17},{2,18},{3,19},{4,20},{5,21},{6,22},{7,23},{8,24},{9,... | collective-permute-start | bytes 589832 | tf_op jit(solution)/shard_map/ppermute | solution.py:222
  33.2 0.6 slice_reduce_fusion.1
  34.3 0.0 copy-done.1
  34.4 0.0 copy-done.7
  34.4 4.4 %states.1 = bf16[32,2,768]{2,1,0:T(2,128)(2,1)} custom-call(f32[2]{0:T(128)S(1)} %copy-done.7, bf16[32,24,256]{2,1,0:T(8,128)(2,1)} %copy-done.1), custom_call_target="tpu_custom_call" | custom-call | tf_op jit(solution)/shard_map/states/pallas_call | solution.py:261
  38.7 7.3 %all-to-all-start.2 = ((bf16[32,2,768]{2,1,0:T(2,128)(2,1)}), bf16[32,2,768]{2,1,0:T(2,128)(2,1)S(1)}, u32[]{:S(2)}, u32[]{:S(2)}) async-start(bf16[32,2,768]{2,1,0:T(2,128)(2,1)} %states.1), calls=%async_computation.2 | async-start | bytes 196608 | tf_op jit(solution)/shard_map/all_to_all | solution.py:271
  46.1 0.0 copy-start.2
  46.1 0.0 copy-start.4
  46.1 0.0 copy-start.5
  46.1 0.0 copy-start.6
  46.1 0.0 collective-permute-done.1.refs_3_
  46.1 0.0 copy-start.9
  46.1 0.7 copy-done.9
  46.8 0.0 copy-done.8
  46.8 15.5 %near.2 = (f32[16,2,48,768]{3,2,1,0:T(8,128)}, f32[3,2,16,768]{3,2,1,0:T(8,128)}) custom-call(f32[2]{0:T(128)S(1)} %copy-done.7, f32[2]{0:T(128)S(1)} %copy-done.8, bf16[32,24,256]{2,1,0:T(8,128)(2,1)} %copy-done.1, bf16[32,24,128]{2,1,0:T(8,128)(2,1)} %copy-done.9, bf16[16,2,48,768]{3,2,1,0:T(8,128)(2,1)} %refs_4_.3), custom_call_target="tpu_custom_call" | custom-call | flops 9663676416 | bytes 8000000 | tf_op jit(solution)/shard_map/near/pallas_call | solution.py:227
  62.3 0.0 all-to-all-done.2.refs_1_
  62.3 0.0 copy-start.3
  62.3 0.0 copy-done.2
  62.3 0.0 copy-done.4
  62.3 0.0 copy-done.5
  62.3 0.0 copy-done.6
  62.3 0.6 copy-done.3
  62.9 4.5 %edge.1 = (f32[2,2,16,768]{3,2,1,0:T(8,128)}, f32[256,128]{1,0:T(8,128)}) custom-call(f32[2]{0:T(128)S(1)} %get-tuple-element.205, bf16[32,2,768]{2,1,0:T(2,128)(2,1)} %copy-done.3, bf16[1536,1536]{1,0:T(8,128)(2,1)} %select_convert_fusion.refs_2_, f32[3,2,16,768]{3,2,1,0:T(8,128)} %get-tuple-element.67.refs_3_), custom_call_target="tpu_custom_call" | custom-call | tf_op jit(solution)/shard_map/edge/pallas_call | solution.py:283
  67.4 14.7 %all-to-all-start.3 = ((f32[256,1,128]{2,1,0:T(1,128)}), f32[256,1,128]{2,1,0:T(1,128)S(1)}, u32[]{:S(2)}, u32[]{:S(2)}) async-start(f32[256,1,128]{2,1,0:T(1,128)} %bitcast.28), calls=%async_computation.3 | async-start | bytes 262144 | tf_op jit(solution)/shard_map/all_to_all | solution.py:294
  82.1 4.3 %final.1 = f32[16,2,48,768]{3,2,1,0:T(8,128)} custom-call(f32[2]{0:T(128)S(1)} %get-tuple-element.205, f32[2,2,16,768]{3,2,1,0:T(8,128)} %get-tuple-element.68.edge_ref, f32[16,2,48,768]{3,2,1,0:T(8,128)} %get-tuple-element.69.near_ref), custom_call_target="tpu_custom_call" | custom-call | flops 20000000 | bytes 10000000 | tf_op jit(solution)/shard_map/final/pallas_call | solution.py:298
  86.4 8.8 %all-to-all-done.3 = f32[256,1,128]{2,1,0:T(1,128)S(1)} async-done(((f32[256,1,128]{2,1,0:T(1,128)}), f32[256,1,128]{2,1,0:T(1,128)S(1)}, u32[]{:S(2)}, u32[]{:S(2)}) %all-to-all-start.3) | async-done | bytes 131104 | tf_op jit(solution)/shard_map/all_to_all | solution.py:294
  95.2 0.6 slice_reduce_fusion
  (5 shorter events, 0.1 us)
Async XLA Ops:
  0.6 46.2 %copy-start.8 = (f32[2]{0:T(128)S(1)}, f32[2]{0:T(128)}, u32[]{:S(2)}) copy-start(f32[2]{0:T(128)} %refs_1_.1) | copy-start | bytes 28
  0.6 33.7 %copy-start.7 = (f32[2]{0:T(128)S(1)}, f32[2]{0:T(128)}, u32[]{:S(2)}) copy-start(f32[2]{0:T(128)} %length_x_ref.1) | copy-start | bytes 28
  7.8 23.7 %all-to-all-start.1 = ((bf16[32,24,256]{2,1,0:T(8,128)(2,1)}), bf16[32,24,256]{2,1,0:T(8,128)(2,1)S(1)}, u32[]{:S(2)}, u32[]{:S(2)}) async-start(bf16[32,24,256]{2,1,0:T(8,128)(2,1)} %bucket.2), calls=%async_computation.1 | async-start | bytes 786432 | tf_op jit(solution)/shard_map/all_to_all | solution.py:218
  31.5 2.9 %copy-start.1 = (bf16[32,24,256]{2,1,0:T(8,128)(2,1)}, bf16[32,24,256]{2,1,0:T(8,128)(2,1)S(1)}, u32[]{:S(2)}) copy-start(bf16[32,24,256]{2,1,0:T(8,128)(2,1)S(1)} %all-to-all-done.1.refs_1_.refs_2_) | copy-start | bytes 1179652
  31.5 14.6 %collective-permute-start.1 = (bf16[32,24,128]{2,1,0:T(8,128)(2,1)S(1)}, bf16[32,24,128]{2,1,0:T(8,128)(2,1)S(1)}, u32[]{:S(2)}, u32[]{:S(2)}) collective-permute-start(bf16[32,24,128]{2,1,0:T(8,128)(2,1)S(1)} %slice.12), channel_id=1, source_target_pairs={{0,16},{1,17},{2,18},{3,19},{4,20},{5,21},{6,22},{7,23},{8,24},{9,... | collective-permute-start | bytes 589832 | tf_op jit(solution)/shard_map/ppermute | solution.py:222
  38.7 23.5 %all-to-all-start.2 = ((bf16[32,2,768]{2,1,0:T(2,128)(2,1)}), bf16[32,2,768]{2,1,0:T(2,128)(2,1)S(1)}, u32[]{:S(2)}, u32[]{:S(2)}) async-start(bf16[32,2,768]{2,1,0:T(2,128)(2,1)} %states.1), calls=%async_computation.2 | async-start | bytes 196608 | tf_op jit(solution)/shard_map/all_to_all | solution.py:271
  46.1 16.2 %copy-start.2 = (bf16[16,2048]{1,0:T(8,128)(2,1)S(1)}, bf16[16,2048]{1,0:T(8,128)(2,1)}, u32[]{:S(2)}) copy-start(bf16[16,2048]{1,0:T(8,128)(2,1)} %refs_4_.2) | copy-start | bytes 196612
  46.1 16.2 %copy-start.4 = (s32[2048,1]{0,1:T(1,128)S(1)}, s32[2048,1]{0,1:T(1,128)}, u32[]{:S(2)}) copy-start(s32[2048,1]{0,1:T(1,128)} %param.12) | copy-start | bytes 24580
  46.1 16.2 %copy-start.5 = (s32[2048]{0:T(1024)S(1)}, s32[2048]{0:T(1024)}, u32[]{:S(2)}) copy-start(s32[2048]{0:T(1024)} %param.13) | copy-start | bytes 24580
  46.1 16.2 %copy-start.6 = (f32[2048]{0:T(1024)S(1)}, f32[2048]{0:T(1024)}, u32[]{:S(2)}) copy-start(f32[2048]{0:T(1024)} %param.11) | copy-start | bytes 24580
  46.1 0.7 copy-start.9
  62.3 0.6 copy-start.3
  67.4 27.7 %all-to-all-start.3 = ((f32[256,1,128]{2,1,0:T(1,128)}), f32[256,1,128]{2,1,0:T(1,128)S(1)}, u32[]{:S(2)}, u32[]{:S(2)}) async-start(f32[256,1,128]{2,1,0:T(1,128)} %bitcast.28), calls=%async_computation.3 | async-start | bytes 262144 | tf_op jit(solution)/shard_map/all_to_all | solution.py:294

commit v3 on v2

v3 whole, which is shorter than its diff:
```python
import jax
import jax.numpy as jnp
from jax import lax
from jax.experimental import pallas as pl
from jax.experimental.pallas import tpu as pltpu
from jax.sharding import PartitionSpec as P

CAP = 128
HALF = 64
KEPT = 24
F32 = jnp.float32
BF16 = jnp.bfloat16
LOG2E = 1.4426950408889634
SMEM = pl.BlockSpec(memory_space=pltpu.SMEM)


def iota(shape, dim):
    return lax.broadcasted_iota(jnp.int32, shape, dim)


def room(mib):
    return pltpu.CompilerParams(vmem_limit_bytes=mib * 1024 * 1024)


def flag(mask):
    return mask.astype(F32).astype(BF16)


def dot_last(a, b):
    return lax.dot_general(a, b, (((1,), (1,)), ((), ())), preferred_element_type=F32)


def rates(length):
    return LOG2E / length, 1.0 - (0.5 * LOG2E) * jnp.log(length)


def bucket_body(
    nx, rows, x_block, turn_ref, band_ref, cell_ref, weight_ref, pert_ref, out_ref, slot_ref, data_ref, masked_ref
):
    ends = out_ref.shape[0]
    members, obs = pert_ref.shape
    turn = turn_ref[0]
    earlier = flag(iota((128, 128), 0) < iota((128, 128), 1))
    cell = cell_ref[...]
    band = band_ref[...]
    row = ((cell.astype(F32) + 0.5) * (1.0 / nx)).astype(jnp.int32)
    col = cell - row * nx
    block = ((col.astype(F32) + 0.5) * (1.0 / x_block)).astype(jnp.int32)
    level = (row >= rows // 2).astype(jnp.int32)
    within = col - block * x_block
    data_ref[:members, :] = (weight_ref[...] * pert_ref[...].astype(F32)).astype(BF16)
    pick = iota((data_ref.shape[0] - members, obs), 0)
    coords = jnp.zeros(pick.shape, jnp.int32)
    for at, value in ((0, band), (1, row), (2, within), (4, row), (5, within), (6, block)):
        coords = jnp.where(pick == at, value, coords)
    data_ref[members:, :] = coords.astype(F32).astype(BF16)

    running = jnp.zeros((3 * ends, 1), F32)
    for part in range(obs // 128):
        at = slice(part * 128, (part + 1) * 128)
        key = iota((3 * ends, 128), 0)
        named = ((key == block[:, at] + ends * level[:, at]) | (key == band[:, at] + 2 * ends)).astype(F32)
        before = named * (jnp.dot(named.astype(BF16), earlier, preferred_element_type=F32) + running)
        rank = jnp.sum(before[: 2 * ends], axis=0, keepdims=True).astype(jnp.int32) - turn * HALF
        fits = (rank >= 0) & (rank < HALF)
        slot_ref[0:1, at] = jnp.where(fits, rank + HALF * level[:, at], -1)
        slot_ref[1:2, at] = jnp.sum(before[2 * ends :], axis=0, keepdims=True).astype(jnp.int32)
        running = running + jnp.sum(named, axis=1, keepdims=True)
    counts = running[: 2 * ends].astype(jnp.int32)
    rounds = ((jnp.max(counts, axis=0, keepdims=True) + (HALF - 1)) >> 6).astype(F32)
    filled = jnp.clip(counts - turn * HALF, 0, HALF).astype(F32)

    size = data_ref.shape[0]
    place = iota((KEPT - members, CAP), 0)
    half = iota((1, CAP), 1) < HALF
    for side, dest in ((0, block), (1, band)):
        move = flag(iota((CAP, obs), 0) == slot_ref[side : side + 1, :])
        for end in range(ends):
            masked_ref[end * size : (end + 1) * size, :] = data_ref[...] * flag(dest == end)
        for first in range(0, ends, 8):
            packed = dot_last(masked_ref[first * size : (first + 8) * size, :], move)
            for end in range(first, first + 8):
                own = packed[(end - first) * size : (end - first + 1) * size]
                found = own[members:KEPT]
                if side == 0:
                    out_ref[end, :members, :] = own[:members].astype(BF16)
                    both = jnp.where(half, filled[end : end + 1], filled[ends + end : ends + end + 1])
                    found = jnp.where(place == 3, rounds, jnp.where(place == 7, both, found))
                    out_ref[end, members:KEPT, :] = found.astype(BF16)
                else:
                    out_ref[end, KEPT:, :] = own[:members].astype(BF16)
                    kept = out_ref[end, members:KEPT, :].astype(F32)
                    theirs = (place >= 4) & (place < 7)
                    out_ref[end, members:KEPT, :] = jnp.where(theirs, found, kept).astype(BF16)


def states_body(rows, x_block, length_ref, got_ref, out_ref, a_ref, obs_ref):
    srcs = got_ref.shape[0]
    members = a_ref.shape[0] // rows
    for src in range(srcs):
        at = pl.ds(src * CAP, CAP)
        got = got_ref[src].astype(F32)
        row = got[members + 4 : members + 5]
        obs_ref[0:3, at] = got[members + 4 : members + 7]
        here = iota((rows, CAP), 0).astype(F32) == row
        for k in range(members):
            payload = got[KEPT + k : KEPT + k + 1]
            a_ref[k * rows : (k + 1) * rows, at] = jnp.where(here, payload, 0.0).astype(BF16)
    length = jnp.where(obs_ref[0:1, :] >= rows // 2, length_ref[1], length_ref[0])
    rate, scale = rates(length)
    within = obs_ref[1:2, :]
    place = iota((2 * srcs, srcs * CAP), 0)
    right = (place & 1) == 1
    ahead = (place >> 1) - obs_ref[2:3, :].astype(jnp.int32)
    steps = jnp.where(right, -ahead, ahead) & (srcs - 1)
    gap = (steps * x_block).astype(F32) + jnp.where(right, within - (x_block - 1.0), -within)
    apart = (steps >= 1) & (steps < srcs // 2)
    edge = jnp.where(apart, jnp.exp2(scale - jnp.maximum(gap, 0.0) * rate), 0.0).astype(BF16)
    value = dot_last(edge, a_ref[...]).astype(BF16)
    for block in range(srcs):
        out_ref[block] = value[2 * block : 2 * block + 2]


def decays(length, shape):
    rate = LOG2E / jnp.full(shape, length, F32)
    x = iota(shape, 0).astype(F32)
    return jnp.exp2(-x * rate), jnp.exp2((x - (shape[0] - 1.0)) * rate)


def filter_body(rows, length_ref, out_ref):
    some, ny = out_ref.shape
    at = iota((some, 128), 0) + pl.program_id(0) * some
    band = ((at.astype(F32) + 0.5) * (1.0 / rows)).astype(jnp.int32)
    row = at - band * rows
    level = (row >= rows // 2).astype(jnp.int32)
    y = (band * (rows // 2) + row - level * (rows // 2)).astype(F32)[:, :1]
    rate, scale = rates(jnp.where(level == 1, length_ref[1], length_ref[0]))
    gap = jnp.abs(iota((some, ny), 1).astype(F32) - y)
    out_ref[...] = jnp.exp2(scale[:, :1] - gap * rate[:, :1]).astype(BF16)


def near_body(
    ny_loc,
    nx,
    length_x_ref,
    length_y_ref,
    own_ref,
    far_ref,
    base_ref,
    out_ref,
    moments_ref,
    rounds_ref,
    obs_ref,
    total_ref,
    count_ref,
    scalar_ref,
    *buffers,
):
    srcs = own_ref.shape[0]
    members, _, cols, ny = out_ref.shape
    level = pl.program_id(0)
    lane = iota((KEPT, CAP), 1)
    last = iota((KEPT, CAP), 0) == KEPT - 1

    @pl.when(level == 0)
    def _():
        most = jnp.zeros((8, CAP), F32)
        for which, ref in enumerate((own_ref, far_ref)):
            for src in range(srcs):
                coords = ref[src, members:KEPT, :].astype(F32)
                at = which * srcs + src
                count_ref[at : at + 1, :] = coords[7:8].astype(jnp.int32)
                most = jnp.maximum(most, coords)
        rounds_ref[0] = jnp.max(jnp.where(iota((8, CAP), 0) == 3, most, 0.0)).astype(jnp.int32)
        pltpu.sync_copy(count_ref, scalar_ref)

    filled = jnp.int32(0)
    now = jnp.zeros((KEPT, CAP), F32)
    for which, ref in enumerate((own_ref, far_ref)):
        for src in range(srcs):
            count = scalar_ref[which * srcs + src, level * HALF]
            start = filled & (CAP - 1)
            value = jnp.where(last, float(which), ref[src].astype(F32))
            value = pltpu.roll(value, (start - level * HALF) & (CAP - 1), 1)
            valid = ((lane - start) & (CAP - 1)) < count
            now = jnp.where(valid & (lane >= start), value, now)
            obs_ref[filled >> 7] = now
            now = jnp.where(start + count >= CAP, jnp.where(valid & (lane < start), value, 0.0), now)
            filled = filled + count
    obs_ref[filled >> 7] = now
    for more in range(1, 7):
        obs_ref[(filled >> 7) + more] = jnp.zeros((KEPT, CAP), F32)

    def constants(ref, shape):
        rate, scale = rates(jnp.full((8, CAP), ref[level], F32))
        return jnp.broadcast_to(rate[:1], shape), jnp.broadcast_to(scale[:1], shape)

    rate_x, scale_x = constants(length_x_ref, (1, CAP))
    rate_y, scale_y = constants(length_y_ref, (1, CAP))
    step = 2 * CAP

    def build(which, a_ref, fy_ref):
        for piece in range(2):
            at = slice(piece * CAP, (piece + 1) * CAP)
            slots = obs_ref[2 * which + piece]
            opposite = slots[KEPT - 1 : KEPT]
            gap = jnp.abs(iota((cols, CAP), 0).astype(F32) - slots[members + 2 : members + 3])
            gap = opposite * (nx // 2) + (1.0 - 2.0 * opposite) * gap
            filter_x = jnp.exp2(scale_x - gap * rate_x)
            for k in range(members):
                a_ref[k * cols : (k + 1) * cols, at] = (filter_x * slots[k : k + 1]).astype(BF16)
            row = slots[members + 1 : members + 2] - (level * ny_loc).astype(F32)
            y = slots[members : members + 1] * ny_loc + jnp.maximum(row, 0.0)
            gap = jnp.abs(iota((ny, CAP), 0).astype(F32) - y)
            fy_ref[:, at] = jnp.exp2(scale_y - gap * rate_y).astype(BF16)

    one, two = buffers[:2], buffers[2:]
    total_ref[...] = jnp.zeros(total_ref.shape, F32)
    build(0, *one)

    def pair(i, carry):
        build(2 * i + 1, *two)
        total_ref[...] = total_ref[...] + dot_last(one[0][...], one[1][...])
        build(2 * i + 2, *one)
        total_ref[...] = total_ref[...] + dot_last(two[0][...], two[1][...])
        return carry

    lax.fori_loop(0, (filled + (2 * step - 1)) >> 9, pair, 0)

    left, right = decays(length_x_ref[level], (cols, ny))
    for k in range(members):
        value = base_ref[k, 0].astype(F32) + total_ref[k * cols : (k + 1) * cols, :]
        out_ref[k, 0] = value
        for which, factor in enumerate((left, right, value)):
            moments_ref[which, 0, k : k + 1] = jnp.sum(value * factor, axis=0, keepdims=True)


def edge_body(cols, length_x_ref, got_ref, fy_ref, level_ref, moments_ref, out_ref, sum_ref, lhs_ref):
    bands, _, lanes = got_ref.shape
    _, levels, members, ny = out_ref.shape
    rows = lanes // members
    got = [got_ref[b].astype(F32) for b in range(bands)]
    for k in range(members):
        piece = jnp.concatenate([got[b][:, k * rows : (k + 1) * rows] for b in range(bands)], axis=1)
        lhs_ref[k : k + 1, :] = piece[0:1]
        lhs_ref[members + k : members + k + 1, :] = piece[1:2]
    lhs = lhs_ref[...]
    level_of = level_ref[0:1, :]
    lhs = jnp.concatenate([jnp.where(level_of == level, lhs, 0.0).astype(BF16) for level in range(levels)], axis=0)
    edge = jnp.dot(lhs, fy_ref[...], preferred_element_type=F32)
    total = jnp.zeros((members, ny), F32)
    for level in range(levels):
        at = 2 * level * members
        one, two = edge[at : at + members], edge[at + members : at + 2 * members]
        out_ref[0, level], out_ref[1, level] = one, two
        left, right = decays(length_x_ref[level], (cols, 128))

        def over_columns(value):
            return jnp.sum(value, axis=0, keepdims=True)[:, :1]

        total = total + moments_ref[2, level]
        total = total + one * (2.0 * moments_ref[0, level] + one * over_columns(left * left))
        total = total + two * (2.0 * moments_ref[1, level] + two * over_columns(right * right))
        total = total + one * two * (2.0 * over_columns(left * right))
    sum_ref[...] = jnp.full(sum_ref.shape, jnp.sum(total), F32)


def final_body(length_x_ref, edge_ref, near_ref, out_ref):
    part, levels, cols, ny = out_ref.shape
    for level in range(levels):
        left, right = decays(length_x_ref[level], (cols, ny))
        for k in range(part):
            one, two = edge_ref[0, level, k : k + 1], edge_ref[1, level, k : k + 1]
            out_ref[k, level] = near_ref[k, level] + left * one + right * two


def on_device(control, member_pert, obs_weight, obs_band, obs_cell, length_x, length_y):
    members, levels, x_block, ny = control.shape
    bands = lax.axis_size("band")
    groups = lax.axis_size("mem")
    ny_loc = ny // bands
    nx = x_block * bands
    obs = obs_cell.shape[0]
    rows = levels * ny_loc
    size = 32

    def route(turn, beside=None):
        packed = pl.pallas_call(
            lambda *refs: bucket_body(nx, rows, x_block, *refs),
            in_specs=[SMEM] + [pl.BlockSpec(memory_space=pltpu.VMEM)] * 4,
            out_shape=jax.ShapeDtypeStruct((bands, KEPT + members, CAP), BF16),
            scratch_shapes=[
                pltpu.VMEM((8, obs), jnp.int32),
                pltpu.VMEM((size, obs), BF16),
                pltpu.VMEM((bands * size, obs), BF16),
            ],
            compiler_params=room(16),
            name="bucket",
        )(turn, obs_band.reshape(1, obs), obs_cell.reshape(1, obs), obs_weight.reshape(1, obs), member_pert)
        got = lax.all_to_all(packed, "band", 0, 0, tiled=True)
        if beside is not None:
            got, beside = lax.optimization_barrier((got, beside))
        own = got[:, :KEPT]
        swap = [(i, (i + bands // 2) % bands) for i in range(bands)]
        return got, own, lax.ppermute(own, "band", swap), beside

    def near_field(own, opposite, base):
        by_level = pl.BlockSpec((members, 1, x_block, ny), lambda i: (0, i, 0, 0))
        slots = 2 * bands * HALF
        buffers = [pltpu.VMEM((members * x_block, 2 * CAP), BF16), pltpu.VMEM((ny, 2 * CAP), BF16)]
        return pl.pallas_call(
            lambda *refs: near_body(ny_loc, nx, *refs),
            grid=(levels,),
            in_specs=[
                SMEM,
                SMEM,
                pl.BlockSpec((bands, KEPT, CAP), lambda i: (0, 0, 0)),
                pl.BlockSpec((bands, KEPT, CAP), lambda i: (0, 0, 0)),
                by_level,
            ],
            out_specs=[by_level, pl.BlockSpec((3, 1, members, ny), lambda i: (0, i, 0, 0)), SMEM],
            out_shape=[
                jax.ShapeDtypeStruct((members, levels, x_block, ny), F32),
                jax.ShapeDtypeStruct((3, levels, members, ny), F32),
                jax.ShapeDtypeStruct((1,), jnp.int32),
            ],
            scratch_shapes=[
                pltpu.VMEM((slots // CAP + 8, KEPT, CAP), F32),
                pltpu.VMEM((members * x_block, ny), F32),
                pltpu.VMEM((2 * bands, CAP), jnp.int32),
                pltpu.SMEM((2 * bands, CAP), jnp.int32),
                *buffers,
                *buffers,
            ],
            compiler_params=room(28),
            cost_estimate=pl.CostEstimate(
                flops=levels * members * x_block * slots * ny, bytes_accessed=8_000_000, transcendentals=4_000_000
            ),
            name="near",
        )(length_x, length_y, own, opposite, base)

    some = 8 * rows
    filter_y = pl.pallas_call(
        lambda *refs: filter_body(rows, *refs),
        grid=(bands * rows // some,),
        in_specs=[SMEM],
        out_specs=pl.BlockSpec((some, ny), lambda i: (i, 0)),
        out_shape=jax.ShapeDtypeStruct((bands * rows, ny), BF16),
        compiler_params=room(16),
        cost_estimate=pl.CostEstimate(flops=5_000_000, bytes_accessed=3_000_000, transcendentals=1_200_000),
        name="filter",
    )(length_y)

    got, own, opposite, filter_y = route(jnp.zeros((1,), jnp.int32), filter_y)
    states = pl.pallas_call(
        lambda *refs: states_body(rows, x_block, *refs),
        in_specs=[SMEM, pl.BlockSpec(memory_space=pltpu.VMEM)],
        out_shape=jax.ShapeDtypeStruct((bands, 2, members * rows), BF16),
        scratch_shapes=[pltpu.VMEM((members * rows, bands * CAP), BF16), pltpu.VMEM((8, bands * CAP), F32)],
        compiler_params=room(20),
        name="states",
    )(length_x, got)
    edges = lax.all_to_all(states, "band", 0, 0, tiled=True)

    near, moments, rounds = near_field(own, opposite, control)

    def again(carry):
        turn, near, _ = carry
        _, more, more_opposite, _ = route(turn.reshape(1))
        return (turn + 1, *near_field(more, more_opposite, near)[:2])

    _, near, moments = lax.while_loop(lambda carry: carry[0] < rounds[0], again, (jnp.int32(1), near, moments))

    level_of = jnp.broadcast_to(jnp.arange(bands * rows, dtype=jnp.int32) // ny_loc % levels, (8, bands * rows))
    edge, partial_value = pl.pallas_call(
        lambda *refs: edge_body(x_block, *refs),
        in_specs=[SMEM] + [pl.BlockSpec(memory_space=pltpu.VMEM)] * 4,
        out_shape=[
            jax.ShapeDtypeStruct((2, levels, members, ny), F32),
            jax.ShapeDtypeStruct((groups * bands, 128), F32),
        ],
        scratch_shapes=[pltpu.VMEM((2 * members, bands * rows), F32)],
        compiler_params=room(16),
        name="edge",
    )(length_x, edges, filter_y, level_of, moments)
    partials = lax.all_to_all(partial_value, ("mem", "band"), 0, 0, tiled=True)

    part = 8
    by_member = pl.BlockSpec((part, levels, x_block, ny), lambda i: (i, 0, 0, 0))
    gradient = pl.pallas_call(
        final_body,
        grid=(members // part,),
        in_specs=[SMEM, pl.BlockSpec((2, levels, part, ny), lambda i: (0, 0, i, 0)), by_member],
        out_specs=by_member,
        out_shape=jax.ShapeDtypeStruct((members, levels, x_block, ny), F32),
        compiler_params=room(24),
        cost_estimate=pl.CostEstimate(flops=20_000_000, bytes_accessed=10_000_000, transcendentals=0),
        name="final",
    )(length_x, edge, near)
    gradient_dot = jnp.sum(partials[:, 0]) * (1.0 / (members * groups * levels * ny * nx))
    return (gradient, gradient_dot)


def solution(mesh):
    return jax.shard_map(
        on_device,
        mesh=mesh,
        in_specs=(
            P("mem", None, "band", None),
            P("mem", "band"),
            P("band"),
            P("band", None),
            P("band"),
            P(),
            P(),
        ),
        out_specs=(P("mem", None, "band", None), P()),
        check_vma=False,
    )
```

time: 98 us -> 92.6 us (0.945)
  other arithmetic: 10.7 us -> 0.65 us
  waiting for transfers between devices: 12.3 us -> 16.7 us
    convert_element_type x1 -> x0, other arithmetic: 8.07 us -> none  [on_device(): filter_y = jnp.where(at_level[:, None] == to_level[None, :], 2.0 / jnp.sq...]
    all_to_all x1, waiting for transfers between devices: 3.58 us -> 7.94 us  [route(): got = lax.all_to_all(packed, 'band', 0, 0, tiled=True)]
    pallas_call x1 -> x2, Pallas kernels: 4.37 us -> 6.33 us  [the longest x1 4.1 us: on_device(): pl.pallas_call(lambda *refs: states_body(rows, x_block, *refs), in_specs=...]
    pallas_call x1, Pallas kernels: 4.54 us -> 2.74 us  [on_device(): pl.pallas_call(lambda *refs: edge_body(x_block, *refs), in_specs=[SMEM] +...]
    gather x1 -> x0, other arithmetic: 1.33 us -> none  [on_device(): length = length_y[to_level][None, :]]
    gather x1 -> x0, local copies, waits for them, and re-layouts: 1.32 us -> none  [on_device(): length = length_y[to_level][None, :]]
  transfers between devices with their start and end apart: 4 -> 4, of which waited for: 2 -> 2; matrix products, arithmetic and copies ran while one was open for 9% -> 0% of each run, Pallas kernels for 25% -> 29%
where the time goes in v3:
time: 92.6 us; the launch traced here: 92.3 us
  starting transfers between devices  35.8 us (39%)
  Pallas kernels  34 us (37%)
  waiting for transfers between devices  16.7 us (18%)
  between operations  2.54 us (3%)
  local copies, waits for them, and re-layouts  1.71 us (2%)
    pallas_call x1, Pallas kernels, near_field(): pl.pallas_call(lambda *refs: near_body(ny_loc, nx, *refs), grid=(levels,)...  16.3 us
    all_to_all x1, starting transfers between devices, on_device(): partials = lax.all_to_all(partial_value, ('mem', 'band'), 0, 0, tiled=True)  15 us
    all_to_all x1, starting transfers between devices, route(): got = lax.all_to_all(packed, 'band', 0, 0, tiled=True)  12 us
    all_to_all x1, waiting for transfers between devices, on_device(): partials = lax.all_to_all(partial_value, ('mem', 'band'), 0, 0, tiled=True)  8.81 us
    all_to_all x1, waiting for transfers between devices, route(): got = lax.all_to_all(packed, 'band', 0, 0, tiled=True)  7.94 us
    all_to_all x1, starting transfers between devices, on_device(): edges = lax.all_to_all(states, 'band', 0, 0, tiled=True)  6.87 us
    pallas_call x1, Pallas kernels, route(): pl.pallas_call(lambda *refs: bucket_body(nx, rows, x_block, *refs), in_sp...  4.39 us
    pallas_call x1, Pallas kernels, on_device(): pl.pallas_call(final_body, grid=(members // part,), in_specs=[SMEM, pl.Bl...  4.24 us
  transfers between devices with their start and end apart: 4, of which 2 were waited for; matrix products, arithmetic and copies ran while one was open for 0% of the time, Pallas kernels for 29%

profile of v3, /device:TPU:1, one launch (start us, length us, event | category | flops | bytes accessed | tf_op | source)
XLA Modules:
  0.0 92.3 jit_solution(5117672012222553473)
XLA Ops:
  0.6 4.4 %bucket.2 = bf16[32,40,128]{2,1,0:T(8,128)(2,1)} custom-call(s32[1]{0:T(128)} %constant.25.clone.1.refs_0_, s32[1,2048]{1,0:T(1,128)} %bitcast.22, s32[1,2048]{1,0:T(1,128)} %bitcast.24, f32[1,2048]{1,0:T(1,128)} %bitcast.26, bf16[16,2048]{1,0:T(8,128)(2,1)} %refs_4_.2), custom_call_target="tpu_custom_call" | custom-call | tf_op jit(solution)/shard_map/bucket/pallas_call | solution.py:288
  5.0 12.0 %all-to-all-start.1 = ((bf16[32,40,128]{2,1,0:T(8,128)(2,1)}), bf16[32,40,128]{2,1,0:T(8,128)(2,1)S(1)}, u32[]{:S(2)}, u32[]{:S(2)}) async-start(bf16[32,40,128]{2,1,0:T(8,128)(2,1)} %bucket.2), calls=%async_computation.1 | async-start | bytes 655360 | tf_op jit(solution)/shard_map/all_to_all | solution.py:300
  17.1 2.2 %filter.1.refs_2_ = bf16[1536,768]{1,0:T(8,128)(2,1)S(1)} custom-call(f32[2]{0:T(128)} %refs_1_.1), custom_call_target="tpu_custom_call" | custom-call | flops 5000000 | bytes 3000000 | tf_op jit(solution)/shard_map/filter/pallas_call | solution.py:343
  19.3 7.9 %all-to-all-done.1.refs_1_ = bf16[32,40,128]{2,1,0:T(8,128)(2,1)S(1)} async-done(((bf16[32,40,128]{2,1,0:T(8,128)(2,1)}), bf16[32,40,128]{2,1,0:T(8,128)(2,1)S(1)}, u32[]{:S(2)}, u32[]{:S(2)}) %all-to-all-start.1) | async-done | bytes 327712 | tf_op jit(solution)/shard_map/all_to_all | solution.py:300
  27.3 1.9 %collective-permute-start.1 = (bf16[32,24,128]{2,1,0:T(8,128)(2,1)S(1)}, bf16[32,24,128]{2,1,0:T(8,128)(2,1)S(1)}, u32[]{:S(2)}, u32[]{:S(2)}) collective-permute-start(bf16[32,24,128]{2,1,0:T(8,128)(2,1)S(1)} %slice.9.refs_2_), channel_id=1, source_target_pairs={{0,16},{1,17},{2,18},{3,19},{4,20},{5,21},{6,22},{7,23},{8,24},{9,... | collective-permute-start | bytes 589832 | tf_op jit(solution)/shard_map/ppermute | solution.py:305
  29.1 4.1 %states.1 = bf16[32,2,768]{2,1,0:T(2,128)(2,1)} custom-call(f32[2]{0:T(128)} %length_x_ref.1, bf16[32,40,128]{2,1,0:T(8,128)(2,1)S(1)} %all-to-all-done.1.refs_1_), custom_call_target="tpu_custom_call" | custom-call | tf_op jit(solution)/shard_map/states/pallas_call | solution.py:355
  33.2 6.9 %all-to-all-start.2 = ((bf16[32,2,768]{2,1,0:T(2,128)(2,1)}), bf16[32,2,768]{2,1,0:T(2,128)(2,1)S(1)}, u32[]{:S(2)}, u32[]{:S(2)}) async-start(bf16[32,2,768]{2,1,0:T(2,128)(2,1)} %states.1), calls=%async_computation.2 | async-start | bytes 196608 | tf_op jit(solution)/shard_map/all_to_all | solution.py:363
  40.1 0.0 collective-permute-done.1.refs_3_
  40.1 0.0 copy-start
  40.1 1.7 %copy-done = bf16[16,2,48,768]{3,2,1,0:T(8,128)(2,1)S(1)} copy-done((bf16[16,2,48,768]{3,2,1,0:T(8,128)(2,1)S(1)}, bf16[16,2,48,768]{3,2,1,0:T(8,128)(2,1)}, u32[]{:S(2)}) %copy-start) | copy-done | bytes 2359320
  41.8 0.0 copy-start.1
  41.8 0.0 copy-start.2
  41.8 0.0 copy-start.3
  41.8 0.0 copy-start.4
  41.8 0.0 copy-start.5
  41.8 0.0 copy-start.6
  41.8 16.3 %near.2 = (f32[16,2,48,768]{3,2,1,0:T(8,128)}, f32[3,2,16,768]{3,2,1,0:T(8,128)}, s32[1]{0:T(128)}) custom-call(f32[2]{0:T(128)} %length_x_ref.1, f32[2]{0:T(128)} %refs_1_.1, bf16[32,24,128]{2,1,0:T(8,128)(2,1)S(1)} %slice.9.refs_2_, bf16[32,24,128]{2,1,0:T(8,128)(2,1)S(1)} %collective-permute-done.1.refs_3_, bf16[16,2,48,768]{3,2,1,0:T(8,128)(2,1)S(1)} %copy-done), custom_call_target="tpu_custom_call" | custom-call | flops 4831838208 | bytes 8000000 | tf_op jit(solution)/shard_map/near/pallas_call | solution.py:311
  58.2 0.0 all-to-all-done.2.refs_1_
  58.2 0.0 copy-done.1
  58.2 0.0 copy-done.2
  58.2 0.0 copy-done.3
  58.2 0.0 copy-done.4
  58.2 0.0 copy-done.5
  58.2 0.0 copy-done.6
  58.2 0.8 while.12
  59.1 2.7 %edge.1 = (f32[2,2,16,768]{3,2,1,0:T(8,128)S(1)}, f32[256,128]{1,0:T(8,128)}) custom-call(f32[2]{0:T(128)S(1)} %get-tuple-element.197, bf16[32,2,768]{2,1,0:T(2,128)(2,1)S(1)} %all-to-all-done.2.refs_1_, bf16[1536,768]{1,0:T(8,128)(2,1)S(1)} %filter.1.refs_2_, s32[8,1536]{1,0:T(8,128)S(1)} %broadcast_in_dim.3.refs_3_, ...), custom_call_target="tpu_custom_call" | custom-call | tf_op jit(solution)/shard_map/edge/pallas_call | solution.py:375
  61.8 15.0 %all-to-all-start.3 = ((f32[256,1,128]{2,1,0:T(1,128)}), f32[256,1,128]{2,1,0:T(1,128)S(1)}, u32[]{:S(2)}, u32[]{:S(2)}) async-start(f32[256,1,128]{2,1,0:T(1,128)} %bitcast.9), calls=%async_computation.3 | async-start | bytes 262144 | tf_op jit(solution)/shard_map/all_to_all | solution.py:386
  76.8 4.2 %final.1 = f32[16,2,48,768]{3,2,1,0:T(8,128)} custom-call(f32[2]{0:T(128)S(1)} %get-tuple-element.197, f32[2,2,16,768]{3,2,1,0:T(8,128)S(1)} %get-tuple-element.70.edge_ref, f32[16,2,48,768]{3,2,1,0:T(8,128)} %get-tuple-element.71.near_ref), custom_call_target="tpu_custom_call" | custom-call | flops 20000000 | bytes 10000000 | tf_op jit(solution)/shard_map/final/pallas_call | solution.py:390
  81.1 8.8 %all-to-all-done.3 = f32[256,1,128]{2,1,0:T(1,128)S(1)} async-done(((f32[256,1,128]{2,1,0:T(1,128)}), f32[256,1,128]{2,1,0:T(1,128)S(1)}, u32[]{:S(2)}, u32[]{:S(2)}) %all-to-all-start.3) | async-done | bytes 131104 | tf_op jit(solution)/shard_map/all_to_all | solution.py:386
  89.9 0.6 slice_reduce_fusion
  (3 shorter events, 0.0 us)
Async XLA Ops:
  5.0 22.2 %all-to-all-start.1 = ((bf16[32,40,128]{2,1,0:T(8,128)(2,1)}), bf16[32,40,128]{2,1,0:T(8,128)(2,1)S(1)}, u32[]{:S(2)}, u32[]{:S(2)}) async-start(bf16[32,40,128]{2,1,0:T(8,128)(2,1)} %bucket.2), calls=%async_computation.1 | async-start | bytes 655360 | tf_op jit(solution)/shard_map/all_to_all | solution.py:300
  27.3 12.9 %collective-permute-start.1 = (bf16[32,24,128]{2,1,0:T(8,128)(2,1)S(1)}, bf16[32,24,128]{2,1,0:T(8,128)(2,1)S(1)}, u32[]{:S(2)}, u32[]{:S(2)}) collective-permute-start(bf16[32,24,128]{2,1,0:T(8,128)(2,1)S(1)} %slice.9.refs_2_), channel_id=1, source_target_pairs={{0,16},{1,17},{2,18},{3,19},{4,20},{5,21},{6,22},{7,23},{8,24},{9,... | collective-permute-start | bytes 589832 | tf_op jit(solution)/shard_map/ppermute | solution.py:305
  33.2 24.9 %all-to-all-start.2 = ((bf16[32,2,768]{2,1,0:T(2,128)(2,1)}), bf16[32,2,768]{2,1,0:T(2,128)(2,1)S(1)}, u32[]{:S(2)}, u32[]{:S(2)}) async-start(bf16[32,2,768]{2,1,0:T(2,128)(2,1)} %states.1), calls=%async_computation.2 | async-start | bytes 196608 | tf_op jit(solution)/shard_map/all_to_all | solution.py:363
  40.1 1.7 %copy-start = (bf16[16,2,48,768]{3,2,1,0:T(8,128)(2,1)S(1)}, bf16[16,2,48,768]{3,2,1,0:T(8,128)(2,1)}, u32[]{:S(2)}) copy-start(bf16[16,2,48,768]{3,2,1,0:T(8,128)(2,1)} %refs_4_.3) | copy-start | bytes 7077892
  41.8 16.4 %copy-start.1 = (bf16[16,2048]{1,0:T(8,128)(2,1)S(1)}, bf16[16,2048]{1,0:T(8,128)(2,1)}, u32[]{:S(2)}) copy-start(bf16[16,2048]{1,0:T(8,128)(2,1)} %refs_4_.2) | copy-start | bytes 196612
  41.8 16.4 %copy-start.2 = (s32[2048,1]{0,1:T(1,128)S(1)}, s32[2048,1]{0,1:T(1,128)}, u32[]{:S(2)}) copy-start(s32[2048,1]{0,1:T(1,128)} %param.12) | copy-start | bytes 24580
  41.8 16.4 %copy-start.3 = (s32[2048]{0:T(1024)S(1)}, s32[2048]{0:T(1024)}, u32[]{:S(2)}) copy-start(s32[2048]{0:T(1024)} %param.13) | copy-start | bytes 24580
  41.8 16.4 %copy-start.4 = (f32[2048]{0:T(1024)S(1)}, f32[2048]{0:T(1024)}, u32[]{:S(2)}) copy-start(f32[2048]{0:T(1024)} %param.11) | copy-start | bytes 24580
  41.8 16.4 %copy-start.5 = (f32[2]{0:T(128)S(1)}, f32[2]{0:T(128)}, u32[]{:S(2)}) copy-start(f32[2]{0:T(128)} %length_x_ref.1) | copy-start | bytes 28
  41.8 16.4 %copy-start.6 = (f32[2]{0:T(128)S(1)}, f32[2]{0:T(128)}, u32[]{:S(2)}) copy-start(f32[2]{0:T(128)} %refs_1_.1) | copy-start | bytes 28
  61.8 28.1 %all-to-all-start.3 = ((f32[256,1,128]{2,1,0:T(1,128)}), f32[256,1,128]{2,1,0:T(1,128)S(1)}, u32[]{:S(2)}, u32[]{:S(2)}) async-start(f32[256,1,128]{2,1,0:T(1,128)} %bitcast.9), calls=%async_computation.3 | async-start | bytes 262144 | tf_op jit(solution)/shard_map/all_to_all | solution.py:386

commit v4 on v3

--- a/solution.py
+++ b/solution.py
@@ -8,6 +8,8 @@
 CAP = 128
 HALF = 64
 KEPT = 24
+USUAL = 2304
+WIDE = 256
 F32 = jnp.float32
 BF16 = jnp.bfloat16
 LOG2E = 1.4426950408889634
@@ -154,7 +156,7 @@
     total_ref,
     count_ref,
     scalar_ref,
-    *buffers,
+    a_ref,
 ):
     srcs = own_ref.shape[0]
     members, _, cols, ny = out_ref.shape
@@ -164,21 +166,24 @@
 
     @pl.when(level == 0)
     def _():
-        most = jnp.zeros((8, CAP), F32)
+        most = counts = jnp.zeros((8, CAP), F32)
         for which, ref in enumerate((own_ref, far_ref)):
             for src in range(srcs):
                 coords = ref[src, members:KEPT, :].astype(F32)
-                at = which * srcs + src
-                count_ref[at : at + 1, :] = coords[7:8].astype(jnp.int32)
+                here = (iota((8, CAP), 1) & (HALF - 1)) == which * srcs + src
+                counts = jnp.where(here, coords, counts)
                 most = jnp.maximum(most, coords)
         rounds_ref[0] = jnp.max(jnp.where(iota((8, CAP), 0) == 3, most, 0.0)).astype(jnp.int32)
+        count_ref[0:1, :] = counts[7:8].astype(jnp.int32)
         pltpu.sync_copy(count_ref, scalar_ref)
 
+    for block in range(USUAL // CAP):
+        obs_ref[block] = jnp.zeros((KEPT, CAP), F32)
     filled = jnp.int32(0)
     now = jnp.zeros((KEPT, CAP), F32)
     for which, ref in enumerate((own_ref, far_ref)):
         for src in range(srcs):
-            count = scalar_ref[which * srcs + src, level * HALF]
+            count = scalar_ref[0, level * HALF + which * srcs + src]
             start = filled & (CAP - 1)
             value = jnp.where(last, float(which), ref[src].astype(F32))
             value = pltpu.roll(value, (start - level * HALF) & (CAP - 1), 1)
@@ -188,8 +193,7 @@
             now = jnp.where(start + count >= CAP, jnp.where(valid & (lane < start), value, 0.0), now)
             filled = filled + count
     obs_ref[filled >> 7] = now
-    for more in range(1, 7):
-        obs_ref[(filled >> 7) + more] = jnp.zeros((KEPT, CAP), F32)
+    obs_ref[(filled >> 7) + 1] = jnp.zeros((KEPT, CAP), F32)
 
     def constants(ref, shape):
         rate, scale = rates(jnp.full((8, CAP), ref[level], F32))
@@ -197,35 +201,34 @@
 
     rate_x, scale_x = constants(length_x_ref, (1, CAP))
     rate_y, scale_y = constants(length_y_ref, (1, CAP))
-    step = 2 * CAP
-
-    def build(which, a_ref, fy_ref):
-        for piece in range(2):
-            at = slice(piece * CAP, (piece + 1) * CAP)
-            slots = obs_ref[2 * which + piece]
+    def build(at, blocks):
+        pieces = []
+        for piece, slots in enumerate(blocks):
+            lanes = slice(at + piece * CAP, at + (piece + 1) * CAP)
             opposite = slots[KEPT - 1 : KEPT]
             gap = jnp.abs(iota((cols, CAP), 0).astype(F32) - slots[members + 2 : members + 3])
             gap = opposite * (nx // 2) + (1.0 - 2.0 * opposite) * gap
             filter_x = jnp.exp2(scale_x - gap * rate_x)
             for k in range(members):
-                a_ref[k * cols : (k + 1) * cols, at] = (filter_x * slots[k : k + 1]).astype(BF16)
+                a_ref[k * cols : (k + 1) * cols, lanes] = (filter_x * slots[k : k + 1]).astype(BF16)
             row = slots[members + 1 : members + 2] - (level * ny_loc).astype(F32)
             y = slots[members : members + 1] * ny_loc + jnp.maximum(row, 0.0)
             gap = jnp.abs(iota((ny, CAP), 0).astype(F32) - y)
-            fy_ref[:, at] = jnp.exp2(scale_y - gap * rate_y).astype(BF16)
-
-    one, two = buffers[:2], buffers[2:]
-    total_ref[...] = jnp.zeros(total_ref.shape, F32)
-    build(0, *one)
-
-    def pair(i, carry):
-        build(2 * i + 1, *two)
-        total_ref[...] = total_ref[...] + dot_last(one[0][...], one[1][...])
-        build(2 * i + 2, *one)
-        total_ref[...] = total_ref[...] + dot_last(two[0][...], two[1][...])
+            pieces.append(jnp.exp2(scale_y - gap * rate_y).astype(BF16))
+        size = len(blocks) * CAP
+        return dot_last(a_ref[:, at : at + size], jnp.concatenate(pieces, axis=1))
+
+    total = jnp.zeros(total_ref.shape, F32)
+    for at in range(0, USUAL, WIDE):
+        some = range(at // CAP, min(at + WIDE, USUAL) // CAP)
+        total = total + build(at, [obs_ref[block] for block in some])
+    total_ref[...] = total
+
+    def more(i, carry):
+        total_ref[...] = total_ref[...] + build(0, [obs_ref[2 * i], obs_ref[2 * i + 1]])
         return carry
 
-    lax.fori_loop(0, (filled + (2 * step - 1)) >> 9, pair, 0)
+    lax.fori_loop(USUAL // (2 * CAP), (filled + (2 * CAP - 1)) >> 8, more, 0)
 
     left, right = decays(length_x_ref[level], (cols, ny))
     for k in range(members):
@@ -307,7 +310,6 @@
     def near_field(own, opposite, base):
         by_level = pl.BlockSpec((members, 1, x_block, ny), lambda i: (0, i, 0, 0))
         slots = 2 * bands * HALF
-        buffers = [pltpu.VMEM((members * x_block, 2 * CAP), BF16), pltpu.VMEM((ny, 2 * CAP), BF16)]
         return pl.pallas_call(
             lambda *refs: near_body(ny_loc, nx, *refs),
             grid=(levels,),
@@ -327,12 +329,11 @@
             scratch_shapes=[
                 pltpu.VMEM((slots // CAP + 8, KEPT, CAP), F32),
                 pltpu.VMEM((members * x_block, ny), F32),
-                pltpu.VMEM((2 * bands, CAP), jnp.int32),
-                pltpu.SMEM((2 * bands, CAP), jnp.int32),
-                *buffers,
-                *buffers,
+                pltpu.VMEM((1, CAP), jnp.int32),
+                pltpu.SMEM((1, CAP), jnp.int32),
+                pltpu.VMEM((members * x_block, USUAL), BF16),
             ],
-            compiler_params=room(28),
+            compiler_params=room(52),
             cost_estimate=pl.CostEstimate(
                 flops=levels * members * x_block * slots * ny, bytes_accessed=8_000_000, transcendentals=4_000_000
             ),

time: 92.6 us -> 87.6 us (0.946)
  Pallas kernels: 34 us -> 30.5 us
  local copies, waits for them, and re-layouts: 1.71 us -> 0.06 us
    pallas_call x1, Pallas kernels: 16.3 us -> 12.8 us  [near_field(): pl.pallas_call(lambda *refs: near_body(ny_loc, nx, *refs), grid=(levels,)...]
    unnamed x14 -> x12, local copies, waits for them, and re-layouts: 1.69 us -> 0.04 us
  transfers between devices with their start and end apart: 4 -> 4, of which waited for: 2 -> 2; matrix products, arithmetic and copies ran while one was open for 0% -> 0% of each run, Pallas kernels for 29% -> 27%
where the time goes in v4:
time: 87.6 us; the launch traced here: 87.2 us
  starting transfers between devices  35.8 us (41%)
  Pallas kernels  30.5 us (35%)
  waiting for transfers between devices  16.7 us (19%)
  between operations  2.56 us (3%)
  loops' own time  0.92 us (1%)
    all_to_all x1, starting transfers between devices, on_device(): partials = lax.all_to_all(partial_value, ('mem', 'band'), 0, 0, tiled=True)  14.8 us
    pallas_call x1, Pallas kernels, near_field(): pl.pallas_call(lambda *refs: near_body(ny_loc, nx, *refs), grid=(levels,)...  12.8 us
    all_to_all x1, starting transfers between devices, route(): got = lax.all_to_all(packed, 'band', 0, 0, tiled=True)  12 us
    all_to_all x1, waiting for transfers between devices, on_device(): partials = lax.all_to_all(partial_value, ('mem', 'band'), 0, 0, tiled=True)  8.78 us
    all_to_all x1, waiting for transfers between devices, route(): got = lax.all_to_all(packed, 'band', 0, 0, tiled=True)  7.94 us
    all_to_all x1, starting transfers between devices, on_device(): edges = lax.all_to_all(states, 'band', 0, 0, tiled=True)  7.05 us
    pallas_call x1, Pallas kernels, route(): pl.pallas_call(lambda *refs: bucket_body(nx, rows, x_block, *refs), in_sp...  4.39 us
    pallas_call x1, Pallas kernels, on_device(): pl.pallas_call(final_body, grid=(members // part,), in_specs=[SMEM, pl.Bl...  4.24 us
  transfers between devices with their start and end apart: 4, of which 2 were waited for; matrix products, arithmetic and copies ran while one was open for 0% of the time, Pallas kernels for 27%

profile of v4, /device:TPU:1, one launch (start us, length us, event | category | flops | bytes accessed | tf_op | source)
XLA Modules:
  0.0 87.2 jit_solution(1945469457954118018)
XLA Ops:
  0.6 4.4 %bucket.2 = bf16[32,40,128]{2,1,0:T(8,128)(2,1)} custom-call(s32[1]{0:T(128)} %constant.25.clone.1.refs_0_, s32[1,2048]{1,0:T(1,128)} %bitcast.22, s32[1,2048]{1,0:T(1,128)} %bitcast.24, f32[1,2048]{1,0:T(1,128)} %bitcast.26, bf16[16,2048]{1,0:T(8,128)(2,1)} %refs_4_.2), custom_call_target="tpu_custom_call" | custom-call | tf_op jit(solution)/shard_map/bucket/pallas_call | solution.py:291
  5.0 12.0 %all-to-all-start.1 = ((bf16[32,40,128]{2,1,0:T(8,128)(2,1)}), bf16[32,40,128]{2,1,0:T(8,128)(2,1)S(1)}, u32[]{:S(2)}, u32[]{:S(2)}) async-start(bf16[32,40,128]{2,1,0:T(8,128)(2,1)} %bucket.2), calls=%async_computation.1 | async-start | bytes 655360 | tf_op jit(solution)/shard_map/all_to_all | solution.py:303
  17.1 2.2 %filter.1.refs_2_ = bf16[1536,768]{1,0:T(8,128)(2,1)S(1)} custom-call(f32[2]{0:T(128)} %refs_1_.1), custom_call_target="tpu_custom_call" | custom-call | flops 5000000 | bytes 3000000 | tf_op jit(solution)/shard_map/filter/pallas_call | solution.py:344
  19.3 7.9 %all-to-all-done.1.refs_1_ = bf16[32,40,128]{2,1,0:T(8,128)(2,1)S(1)} async-done(((bf16[32,40,128]{2,1,0:T(8,128)(2,1)}), bf16[32,40,128]{2,1,0:T(8,128)(2,1)S(1)}, u32[]{:S(2)}, u32[]{:S(2)}) %all-to-all-start.1) | async-done | bytes 327712 | tf_op jit(solution)/shard_map/all_to_all | solution.py:303
  27.3 1.9 %collective-permute-start.1 = (bf16[32,24,128]{2,1,0:T(8,128)(2,1)S(1)}, bf16[32,24,128]{2,1,0:T(8,128)(2,1)S(1)}, u32[]{:S(2)}, u32[]{:S(2)}) collective-permute-start(bf16[32,24,128]{2,1,0:T(8,128)(2,1)S(1)} %slice.9.refs_2_), channel_id=1, source_target_pairs={{0,16},{1,17},{2,18},{3,19},{4,20},{5,21},{6,22},{7,23},{8,24},{9,... | collective-permute-start | bytes 589832 | tf_op jit(solution)/shard_map/ppermute | solution.py:308
  29.1 4.1 %states.1 = bf16[32,2,768]{2,1,0:T(2,128)(2,1)} custom-call(f32[2]{0:T(128)} %length_x_ref.1, bf16[32,40,128]{2,1,0:T(8,128)(2,1)S(1)} %all-to-all-done.1.refs_1_), custom_call_target="tpu_custom_call" | custom-call | tf_op jit(solution)/shard_map/states/pallas_call | solution.py:356
  33.2 7.1 %all-to-all-start.2 = ((bf16[32,2,768]{2,1,0:T(2,128)(2,1)}), bf16[32,2,768]{2,1,0:T(2,128)(2,1)S(1)}, u32[]{:S(2)}, u32[]{:S(2)}) async-start(bf16[32,2,768]{2,1,0:T(2,128)(2,1)} %states.1), calls=%async_computation.2 | async-start | bytes 196608 | tf_op jit(solution)/shard_map/all_to_all | solution.py:364
  40.3 0.0 copy-start
  40.3 0.0 copy-start.1
  40.3 0.0 copy-start.2
  40.3 0.0 copy-start.3
  40.3 0.0 copy-start.4
  40.4 0.0 copy-start.5
  40.4 0.0 collective-permute-done.1.refs_3_
  40.4 12.8 %near.2 = (f32[16,2,48,768]{3,2,1,0:T(8,128)}, f32[3,2,16,768]{3,2,1,0:T(8,128)}, s32[1]{0:T(128)}) custom-call(f32[2]{0:T(128)} %length_x_ref.1, f32[2]{0:T(128)} %refs_1_.1, bf16[32,24,128]{2,1,0:T(8,128)(2,1)S(1)} %slice.9.refs_2_, bf16[32,24,128]{2,1,0:T(8,128)(2,1)S(1)} %collective-permute-done.1.refs_3_, bf16[16,2,48,768]{3,2,1,0:T(8,128)(2,1)} %refs_4_.3), custom_call_target="tpu_custom_call" | custom-call | flops 4831838208 | bytes 8000000 | tf_op jit(solution)/shard_map/near/pallas_call | solution.py:313
  53.2 0.0 all-to-all-done.2.refs_1_
  53.2 0.0 copy-done
  53.2 0.0 copy-done.1
  53.2 0.0 copy-done.2
  53.2 0.0 copy-done.3
  53.2 0.0 copy-done.4
  53.3 0.0 copy-done.5
  53.3 0.9 %while.12 = (s32[]{:T(128)}, f32[16,2,48,768]{3,2,1,0:T(8,128)}, f32[3,2,16,768]{3,2,1,0:T(8,128)}, s32[1]{0:T(128)}, s32[2048,1]{0,1:T(1,128)S(1)}, /*index=5*/...) while((s32[]{:T(128)}, f32[16,2,48,768]{3,2,1,0:T(8,128)}, ...), condition=%wide.region_1.0_spmd, body=%wide.region_0.0_spmd.sunk | while | flops 4831838208 | bytes 19272340 | solution.py:373
  54.2 2.7 %edge.1 = (f32[2,2,16,768]{3,2,1,0:T(8,128)S(1)}, f32[256,128]{1,0:T(8,128)}) custom-call(f32[2]{0:T(128)S(1)} %get-tuple-element.197, bf16[32,2,768]{2,1,0:T(2,128)(2,1)S(1)} %all-to-all-done.2.refs_1_, bf16[1536,768]{1,0:T(8,128)(2,1)S(1)} %filter.1.refs_2_, s32[8,1536]{1,0:T(8,128)S(1)} %broadcast_in_dim.3.refs_3_, ...), custom_call_target="tpu_custom_call" | custom-call | tf_op jit(solution)/shard_map/edge/pallas_call | solution.py:376
  56.9 14.8 %all-to-all-start.3 = ((f32[256,1,128]{2,1,0:T(1,128)}), f32[256,1,128]{2,1,0:T(1,128)S(1)}, u32[]{:S(2)}, u32[]{:S(2)}) async-start(f32[256,1,128]{2,1,0:T(1,128)} %bitcast.9), calls=%async_computation.3 | async-start | bytes 262144 | tf_op jit(solution)/shard_map/all_to_all | solution.py:387
  71.8 4.2 %final.1 = f32[16,2,48,768]{3,2,1,0:T(8,128)} custom-call(f32[2]{0:T(128)S(1)} %get-tuple-element.197, f32[2,2,16,768]{3,2,1,0:T(8,128)S(1)} %get-tuple-element.70.edge_ref, f32[16,2,48,768]{3,2,1,0:T(8,128)} %get-tuple-element.71.near_ref), custom_call_target="tpu_custom_call" | custom-call | flops 20000000 | bytes 10000000 | tf_op jit(solution)/shard_map/final/pallas_call | solution.py:391
  76.0 8.8 %all-to-all-done.3 = f32[256,1,128]{2,1,0:T(1,128)S(1)} async-done(((f32[256,1,128]{2,1,0:T(1,128)}), f32[256,1,128]{2,1,0:T(1,128)S(1)}, u32[]{:S(2)}, u32[]{:S(2)}) %all-to-all-start.3) | async-done | bytes 131104 | tf_op jit(solution)/shard_map/all_to_all | solution.py:387
  84.8 0.6 slice_reduce_fusion
  (3 shorter events, 0.0 us)
Async XLA Ops:
  5.0 22.2 %all-to-all-start.1 = ((bf16[32,40,128]{2,1,0:T(8,128)(2,1)}), bf16[32,40,128]{2,1,0:T(8,128)(2,1)S(1)}, u32[]{:S(2)}, u32[]{:S(2)}) async-start(bf16[32,40,128]{2,1,0:T(8,128)(2,1)} %bucket.2), calls=%async_computation.1 | async-start | bytes 655360 | tf_op jit(solution)/shard_map/all_to_all | solution.py:303
  27.3 13.1 %collective-permute-start.1 = (bf16[32,24,128]{2,1,0:T(8,128)(2,1)S(1)}, bf16[32,24,128]{2,1,0:T(8,128)(2,1)S(1)}, u32[]{:S(2)}, u32[]{:S(2)}) collective-permute-start(bf16[32,24,128]{2,1,0:T(8,128)(2,1)S(1)} %slice.9.refs_2_), channel_id=1, source_target_pairs={{0,16},{1,17},{2,18},{3,19},{4,20},{5,21},{6,22},{7,23},{8,24},{9,... | collective-permute-start | bytes 589832 | tf_op jit(solution)/shard_map/ppermute | solution.py:308
  33.2 20.0 %all-to-all-start.2 = ((bf16[32,2,768]{2,1,0:T(2,128)(2,1)}), bf16[32,2,768]{2,1,0:T(2,128)(2,1)S(1)}, u32[]{:S(2)}, u32[]{:S(2)}) async-start(bf16[32,2,768]{2,1,0:T(2,128)(2,1)} %states.1), calls=%async_computation.2 | async-start | bytes 196608 | tf_op jit(solution)/shard_map/all_to_all | solution.py:364
  40.3 12.9 %copy-start = (bf16[16,2048]{1,0:T(8,128)(2,1)S(1)}, bf16[16,2048]{1,0:T(8,128)(2,1)}, u32[]{:S(2)}) copy-start(bf16[16,2048]{1,0:T(8,128)(2,1)} %refs_4_.2) | copy-start | bytes 196612
  40.3 12.9 %copy-start.1 = (s32[2048,1]{0,1:T(1,128)S(1)}, s32[2048,1]{0,1:T(1,128)}, u32[]{:S(2)}) copy-start(s32[2048,1]{0,1:T(1,128)} %param.12) | copy-start | bytes 24580
  40.3 12.9 %copy-start.2 = (s32[2048]{0:T(1024)S(1)}, s32[2048]{0:T(1024)}, u32[]{:S(2)}) copy-start(s32[2048]{0:T(1024)} %param.13) | copy-start | bytes 24580
  40.3 12.9 %copy-start.3 = (f32[2048]{0:T(1024)S(1)}, f32[2048]{0:T(1024)}, u32[]{:S(2)}) copy-start(f32[2048]{0:T(1024)} %param.11) | copy-start | bytes 24580
  40.3 12.9 %copy-start.4 = (f32[2]{0:T(128)S(1)}, f32[2]{0:T(128)}, u32[]{:S(2)}) copy-start(f32[2]{0:T(128)} %length_x_ref.1) | copy-start | bytes 28
  40.4 12.9 %copy-start.5 = (f32[2]{0:T(128)S(1)}, f32[2]{0:T(128)}, u32[]{:S(2)}) copy-start(f32[2]{0:T(128)} %refs_1_.1) | copy-start | bytes 28
  56.9 27.9 %all-to-all-start.3 = ((f32[256,1,128]{2,1,0:T(1,128)}), f32[256,1,128]{2,1,0:T(1,128)S(1)}, u32[]{:S(2)}, u32[]{:S(2)}) async-start(f32[256,1,128]{2,1,0:T(1,128)} %bitcast.9), calls=%async_computation.3 | async-start | bytes 262144 | tf_op jit(solution)/shard_map/all_to_all | solution.py:387

commit v5 on v4

--- a/solution.py
+++ b/solution.py
@@ -51,7 +51,7 @@
     level = (row >= rows // 2).astype(jnp.int32)
     within = col - block * x_block
     data_ref[:members, :] = (weight_ref[...] * pert_ref[...].astype(F32)).astype(BF16)
-    pick = iota((data_ref.shape[0] - members, obs), 0)
+    pick = iota((data_ref.shape[0] - members, obs), 0) & (KEPT - members - 1)
     coords = jnp.zeros(pick.shape, jnp.int32)
     for at, value in ((0, band), (1, row), (2, within), (4, row), (5, within), (6, block)):
         coords = jnp.where(pick == at, value, coords)
@@ -72,25 +72,34 @@
     rounds = ((jnp.max(counts, axis=0, keepdims=True) + (HALF - 1)) >> 6).astype(F32)
     filled = jnp.clip(counts - turn * HALF, 0, HALF).astype(F32)
 
-    size = data_ref.shape[0]
-    place = iota((KEPT - members, CAP), 0)
+    extra = KEPT - members
+    size = 2 * KEPT
+    place = iota((extra, CAP), 0)
     half = iota((1, CAP), 1) < HALF
+    upper = iota((2 * extra, obs), 0) < extra
     for side, dest in ((0, block), (1, band)):
         move = flag(iota((CAP, obs), 0) == slot_ref[side : side + 1, :])
-        for end in range(ends):
-            masked_ref[end * size : (end + 1) * size, :] = data_ref[...] * flag(dest == end)
+        for end in range(0, ends, 2):
+            at = end // 2 * size
+            one, two = flag(dest == end), flag(dest == end + 1)
+            masked_ref[at : at + members, :] = data_ref[:members, :] * one
+            masked_ref[at + members : at + 2 * members, :] = data_ref[:members, :] * two
+            either = flag(dest == jnp.where(upper, end, end + 1))
+            masked_ref[at + 2 * members : at + size, :] = data_ref[members:, :] * either
         for first in range(0, ends, 8):
-            packed = dot_last(masked_ref[first * size : (first + 8) * size, :], move)
+            packed = dot_last(masked_ref[first // 2 * size : (first // 2 + 4) * size, :], move)
             for end in range(first, first + 8):
-                own = packed[(end - first) * size : (end - first + 1) * size]
-                found = own[members:KEPT]
+                at = (end - first) // 2 * size
+                own = packed[at + end % 2 * members : at + end % 2 * members + members]
+                at = at + 2 * members + end % 2 * extra
+                found = packed[at : at + extra]
                 if side == 0:
-                    out_ref[end, :members, :] = own[:members].astype(BF16)
+                    out_ref[end, :members, :] = own.astype(BF16)
                     both = jnp.where(half, filled[end : end + 1], filled[ends + end : ends + end + 1])
                     found = jnp.where(place == 3, rounds, jnp.where(place == 7, both, found))
                     out_ref[end, members:KEPT, :] = found.astype(BF16)
                 else:
-                    out_ref[end, KEPT:, :] = own[:members].astype(BF16)
+                    out_ref[end, KEPT:, :] = own.astype(BF16)
                     kept = out_ref[end, members:KEPT, :].astype(F32)
                     theirs = (place >= 4) & (place < 7)
                     out_ref[end, members:KEPT, :] = jnp.where(theirs, found, kept).astype(BF16)
@@ -99,26 +108,31 @@
 def states_body(rows, x_block, length_ref, got_ref, out_ref, a_ref, obs_ref):
     srcs = got_ref.shape[0]
     members = a_ref.shape[0] // rows
-    for src in range(srcs):
-        at = pl.ds(src * CAP, CAP)
-        got = got_ref[src].astype(F32)
-        row = got[members + 4 : members + 5]
-        obs_ref[0:3, at] = got[members + 4 : members + 7]
-        here = iota((rows, CAP), 0).astype(F32) == row
-        for k in range(members):
-            payload = got[KEPT + k : KEPT + k + 1]
-            a_ref[k * rows : (k + 1) * rows, at] = jnp.where(here, payload, 0.0).astype(BF16)
-    length = jnp.where(obs_ref[0:1, :] >= rows // 2, length_ref[1], length_ref[0])
-    rate, scale = rates(length)
-    within = obs_ref[1:2, :]
-    place = iota((2 * srcs, srcs * CAP), 0)
-    right = (place & 1) == 1
-    ahead = (place >> 1) - obs_ref[2:3, :].astype(jnp.int32)
-    steps = jnp.where(right, -ahead, ahead) & (srcs - 1)
-    gap = (steps * x_block).astype(F32) + jnp.where(right, within - (x_block - 1.0), -within)
-    apart = (steps >= 1) & (steps < srcs // 2)
-    edge = jnp.where(apart, jnp.exp2(scale - jnp.maximum(gap, 0.0) * rate), 0.0).astype(BF16)
-    value = dot_last(edge, a_ref[...]).astype(BF16)
+    group = 4
+    value = jnp.zeros((2 * srcs, members * rows), F32)
+    for first in range(0, srcs, group):
+        lanes = slice(first * CAP, (first + group) * CAP)
+        for src in range(first, first + group):
+            at = slice(src * CAP, (src + 1) * CAP)
+            got = got_ref[src].astype(F32)
+            row = got[members + 4 : members + 5]
+            obs_ref[0:3, at] = got[members + 4 : members + 7]
+            here = iota((rows, CAP), 0).astype(F32) == row
+            for k in range(members):
+                payload = got[KEPT + k : KEPT + k + 1]
+                a_ref[k * rows : (k + 1) * rows, at] = jnp.where(here, payload, 0.0).astype(BF16)
+        length = jnp.where(obs_ref[0:1, lanes] >= rows // 2, length_ref[1], length_ref[0])
+        rate, scale = rates(length)
+        within = obs_ref[1:2, lanes]
+        place = iota((2 * srcs, group * CAP), 0)
+        right = (place & 1) == 1
+        ahead = (place >> 1) - obs_ref[2:3, lanes].astype(jnp.int32)
+        steps = jnp.where(right, -ahead, ahead) & (srcs - 1)
+        gap = (steps * x_block).astype(F32) + jnp.where(right, within - (x_block - 1.0), -within)
+        apart = (steps >= 1) & (steps < srcs // 2)
+        edge = jnp.where(apart, jnp.exp2(scale - jnp.maximum(gap, 0.0) * rate), 0.0).astype(BF16)
+        value = value + dot_last(edge, a_ref[:, lanes])
+    value = value.astype(BF16)
     for block in range(srcs):
         out_ref[block] = value[2 * block : 2 * block + 2]
 
@@ -285,7 +299,7 @@
     nx = x_block * bands
     obs = obs_cell.shape[0]
     rows = levels * ny_loc
-    size = 32
+    size = 2 * (KEPT - members)
 
     def route(turn, beside=None):
         packed = pl.pallas_call(
@@ -294,8 +308,8 @@
             out_shape=jax.ShapeDtypeStruct((bands, KEPT + members, CAP), BF16),
             scratch_shapes=[
                 pltpu.VMEM((8, obs), jnp.int32),
-                pltpu.VMEM((size, obs), BF16),
-                pltpu.VMEM((bands * size, obs), BF16),
+                pltpu.VMEM((members + size, obs), BF16),
+                pltpu.VMEM((bands * KEPT, obs), BF16),
             ],
             compiler_params=room(16),
             name="bucket",

time: 87.6 us -> 87 us (level)
  no operation moved by 1% of the time
where the time goes in v5:
time: 87 us; the launch traced here: 86.6 us
  starting transfers between devices  35.8 us (41%)
  Pallas kernels  29.9 us (34%)
  waiting for transfers between devices  16.7 us (19%)
  between operations  2.56 us (3%)
  loops' own time  0.92 us (1%)
    all_to_all x1, starting transfers between devices, on_device(): partials = lax.all_to_all(partial_value, ('mem', 'band'), 0, 0, tiled=True)  14.9 us
    pallas_call x1, Pallas kernels, near_field(): pl.pallas_call(lambda *refs: near_body(ny_loc, nx, *refs), grid=(levels,)...  12.8 us
    all_to_all x1, starting transfers between devices, route(): got = lax.all_to_all(packed, 'band', 0, 0, tiled=True)  12 us
    all_to_all x1, waiting for transfers between devices, on_device(): partials = lax.all_to_all(partial_value, ('mem', 'band'), 0, 0, tiled=True)  8.78 us
    all_to_all x1, waiting for transfers between devices, route(): got = lax.all_to_all(packed, 'band', 0, 0, tiled=True)  7.92 us
    all_to_all x1, starting transfers between devices, on_device(): edges = lax.all_to_all(states, 'band', 0, 0, tiled=True)  7.05 us
    pallas_call x1, Pallas kernels, on_device(): pl.pallas_call(final_body, grid=(members // part,), in_specs=[SMEM, pl.Bl...  4.24 us
    pallas_call x1, Pallas kernels, route(): pl.pallas_call(lambda *refs: bucket_body(nx, rows, x_block, *refs), in_sp...  4 us
  transfers between devices with their start and end apart: 4, of which 2 were waited for; matrix products, arithmetic and copies ran while one was open for 0% of the time, Pallas kernels for 27%

profile of v5, /device:TPU:1, one launch (start us, length us, event | category | flops | bytes accessed | tf_op | source)
XLA Modules:
  0.0 86.6 jit_solution(15237892813855477829)
XLA Ops:
  0.6 4.0 %bucket.2 = bf16[32,40,128]{2,1,0:T(8,128)(2,1)} custom-call(s32[1]{0:T(128)} %constant.25.clone.1.refs_0_, s32[1,2048]{1,0:T(1,128)} %bitcast.22, s32[1,2048]{1,0:T(1,128)} %bitcast.24, f32[1,2048]{1,0:T(1,128)} %bitcast.26, bf16[16,2048]{1,0:T(8,128)(2,1)} %refs_4_.2), custom_call_target="tpu_custom_call" | custom-call | tf_op jit(solution)/shard_map/bucket/pallas_call | solution.py:305
  4.6 12.0 %all-to-all-start.1 = ((bf16[32,40,128]{2,1,0:T(8,128)(2,1)}), bf16[32,40,128]{2,1,0:T(8,128)(2,1)S(1)}, u32[]{:S(2)}, u32[]{:S(2)}) async-start(bf16[32,40,128]{2,1,0:T(8,128)(2,1)} %bucket.2), calls=%async_computation.1 | async-start | bytes 655360 | tf_op jit(solution)/shard_map/all_to_all | solution.py:317
  16.7 2.2 %filter.1.refs_2_ = bf16[1536,768]{1,0:T(8,128)(2,1)S(1)} custom-call(f32[2]{0:T(128)} %refs_1_.1), custom_call_target="tpu_custom_call" | custom-call | flops 5000000 | bytes 3000000 | tf_op jit(solution)/shard_map/filter/pallas_call | solution.py:358
  18.9 7.9 %all-to-all-done.1.refs_1_ = bf16[32,40,128]{2,1,0:T(8,128)(2,1)S(1)} async-done(((bf16[32,40,128]{2,1,0:T(8,128)(2,1)}), bf16[32,40,128]{2,1,0:T(8,128)(2,1)S(1)}, u32[]{:S(2)}, u32[]{:S(2)}) %all-to-all-start.1) | async-done | bytes 327712 | tf_op jit(solution)/shard_map/all_to_all | solution.py:317
  26.9 1.9 %collective-permute-start.1 = (bf16[32,24,128]{2,1,0:T(8,128)(2,1)S(1)}, bf16[32,24,128]{2,1,0:T(8,128)(2,1)S(1)}, u32[]{:S(2)}, u32[]{:S(2)}) collective-permute-start(bf16[32,24,128]{2,1,0:T(8,128)(2,1)S(1)} %slice.9.refs_2_), channel_id=1, source_target_pairs={{0,16},{1,17},{2,18},{3,19},{4,20},{5,21},{6,22},{7,23},{8,24},{9,... | collective-permute-start | bytes 589832 | tf_op jit(solution)/shard_map/ppermute | solution.py:322
  28.7 3.9 %states.1 = bf16[32,2,768]{2,1,0:T(2,128)(2,1)} custom-call(f32[2]{0:T(128)} %length_x_ref.1, bf16[32,40,128]{2,1,0:T(8,128)(2,1)S(1)} %all-to-all-done.1.refs_1_), custom_call_target="tpu_custom_call" | custom-call | tf_op jit(solution)/shard_map/states/pallas_call | solution.py:370
  32.6 7.0 %all-to-all-start.2 = ((bf16[32,2,768]{2,1,0:T(2,128)(2,1)}), bf16[32,2,768]{2,1,0:T(2,128)(2,1)S(1)}, u32[]{:S(2)}, u32[]{:S(2)}) async-start(bf16[32,2,768]{2,1,0:T(2,128)(2,1)} %states.1), calls=%async_computation.2 | async-start | bytes 196608 | tf_op jit(solution)/shard_map/all_to_all | solution.py:378
  39.7 0.0 copy-start
  39.7 0.0 copy-start.1
  39.7 0.0 copy-start.2
  39.7 0.0 copy-start.3
  39.7 0.0 copy-start.4
  39.7 0.0 copy-start.5
  39.7 0.0 collective-permute-done.1.refs_3_
  39.7 12.8 %near.2 = (f32[16,2,48,768]{3,2,1,0:T(8,128)}, f32[3,2,16,768]{3,2,1,0:T(8,128)}, s32[1]{0:T(128)}) custom-call(f32[2]{0:T(128)} %length_x_ref.1, f32[2]{0:T(128)} %refs_1_.1, bf16[32,24,128]{2,1,0:T(8,128)(2,1)S(1)} %slice.9.refs_2_, bf16[32,24,128]{2,1,0:T(8,128)(2,1)S(1)} %collective-permute-done.1.refs_3_, bf16[16,2,48,768]{3,2,1,0:T(8,128)(2,1)} %refs_4_.3), custom_call_target="tpu_custom_call" | custom-call | flops 4831838208 | bytes 8000000 | tf_op jit(solution)/shard_map/near/pallas_call | solution.py:327
  52.6 0.0 all-to-all-done.2.refs_1_
  52.6 0.0 copy-done
  52.6 0.0 copy-done.1
  52.6 0.0 copy-done.2
  52.6 0.0 copy-done.3
  52.6 0.0 copy-done.4
  52.6 0.0 copy-done.5
  52.6 0.9 %while.12 = (s32[]{:T(128)}, f32[16,2,48,768]{3,2,1,0:T(8,128)}, f32[3,2,16,768]{3,2,1,0:T(8,128)}, s32[1]{0:T(128)}, s32[2048,1]{0,1:T(1,128)S(1)}, /*index=5*/...) while((s32[]{:T(128)}, f32[16,2,48,768]{3,2,1,0:T(8,128)}, ...), condition=%wide.region_1.0_spmd, body=%wide.region_0.0_spmd.sunk | while | flops 4831838208 | bytes 19272340 | solution.py:387
  53.6 2.7 %edge.1 = (f32[2,2,16,768]{3,2,1,0:T(8,128)S(1)}, f32[256,128]{1,0:T(8,128)}) custom-call(f32[2]{0:T(128)S(1)} %get-tuple-element.197, bf16[32,2,768]{2,1,0:T(2,128)(2,1)S(1)} %all-to-all-done.2.refs_1_, bf16[1536,768]{1,0:T(8,128)(2,1)S(1)} %filter.1.refs_2_, s32[8,1536]{1,0:T(8,128)S(1)} %broadcast_in_dim.3.refs_3_, ...), custom_call_target="tpu_custom_call" | custom-call | tf_op jit(solution)/shard_map/edge/pallas_call | solution.py:390
  56.3 14.9 %all-to-all-start.3 = ((f32[256,1,128]{2,1,0:T(1,128)}), f32[256,1,128]{2,1,0:T(1,128)S(1)}, u32[]{:S(2)}, u32[]{:S(2)}) async-start(f32[256,1,128]{2,1,0:T(1,128)} %bitcast.9), calls=%async_computation.3 | async-start | bytes 262144 | tf_op jit(solution)/shard_map/all_to_all | solution.py:401
  71.2 4.2 %final.1 = f32[16,2,48,768]{3,2,1,0:T(8,128)} custom-call(f32[2]{0:T(128)S(1)} %get-tuple-element.197, f32[2,2,16,768]{3,2,1,0:T(8,128)S(1)} %get-tuple-element.70.edge_ref, f32[16,2,48,768]{3,2,1,0:T(8,128)} %get-tuple-element.71.near_ref), custom_call_target="tpu_custom_call" | custom-call | flops 20000000 | bytes 10000000 | tf_op jit(solution)/shard_map/final/pallas_call | solution.py:405
  75.4 8.8 %all-to-all-done.3 = f32[256,1,128]{2,1,0:T(1,128)S(1)} async-done(((f32[256,1,128]{2,1,0:T(1,128)}), f32[256,1,128]{2,1,0:T(1,128)S(1)}, u32[]{:S(2)}, u32[]{:S(2)}) %all-to-all-start.3) | async-done | bytes 131104 | tf_op jit(solution)/shard_map/all_to_all | solution.py:401
  84.2 0.6 slice_reduce_fusion
  (3 shorter events, 0.0 us)
Async XLA Ops:
  4.6 22.2 %all-to-all-start.1 = ((bf16[32,40,128]{2,1,0:T(8,128)(2,1)}), bf16[32,40,128]{2,1,0:T(8,128)(2,1)S(1)}, u32[]{:S(2)}, u32[]{:S(2)}) async-start(bf16[32,40,128]{2,1,0:T(8,128)(2,1)} %bucket.2), calls=%async_computation.1 | async-start | bytes 655360 | tf_op jit(solution)/shard_map/all_to_all | solution.py:317
  26.9 12.9 %collective-permute-start.1 = (bf16[32,24,128]{2,1,0:T(8,128)(2,1)S(1)}, bf16[32,24,128]{2,1,0:T(8,128)(2,1)S(1)}, u32[]{:S(2)}, u32[]{:S(2)}) collective-permute-start(bf16[32,24,128]{2,1,0:T(8,128)(2,1)S(1)} %slice.9.refs_2_), channel_id=1, source_target_pairs={{0,16},{1,17},{2,18},{3,19},{4,20},{5,21},{6,22},{7,23},{8,24},{9,... | collective-permute-start | bytes 589832 | tf_op jit(solution)/shard_map/ppermute | solution.py:322
  32.6 20.0 %all-to-all-start.2 = ((bf16[32,2,768]{2,1,0:T(2,128)(2,1)}), bf16[32,2,768]{2,1,0:T(2,128)(2,1)S(1)}, u32[]{:S(2)}, u32[]{:S(2)}) async-start(bf16[32,2,768]{2,1,0:T(2,128)(2,1)} %states.1), calls=%async_computation.2 | async-start | bytes 196608 | tf_op jit(solution)/shard_map/all_to_all | solution.py:378
  39.7 12.9 %copy-start = (bf16[16,2048]{1,0:T(8,128)(2,1)S(1)}, bf16[16,2048]{1,0:T(8,128)(2,1)}, u32[]{:S(2)}) copy-start(bf16[16,2048]{1,0:T(8,128)(2,1)} %refs_4_.2) | copy-start | bytes 196612
  39.7 12.9 %copy-start.1 = (s32[2048,1]{0,1:T(1,128)S(1)}, s32[2048,1]{0,1:T(1,128)}, u32[]{:S(2)}) copy-start(s32[2048,1]{0,1:T(1,128)} %param.12) | copy-start | bytes 24580
  39.7 12.9 %copy-start.2 = (s32[2048]{0:T(1024)S(1)}, s32[2048]{0:T(1024)}, u32[]{:S(2)}) copy-start(s32[2048]{0:T(1024)} %param.13) | copy-start | bytes 24580
  39.7 12.9 %copy-start.3 = (f32[2048]{0:T(1024)S(1)}, f32[2048]{0:T(1024)}, u32[]{:S(2)}) copy-start(f32[2048]{0:T(1024)} %param.11) | copy-start | bytes 24580
  39.7 12.9 %copy-start.4 = (f32[2]{0:T(128)S(1)}, f32[2]{0:T(128)}, u32[]{:S(2)}) copy-start(f32[2]{0:T(128)} %length_x_ref.1) | copy-start | bytes 28
  39.7 12.9 %copy-start.5 = (f32[2]{0:T(128)S(1)}, f32[2]{0:T(128)}, u32[]{:S(2)}) copy-start(f32[2]{0:T(128)} %refs_1_.1) | copy-start | bytes 28
  56.3 27.9 %all-to-all-start.3 = ((f32[256,1,128]{2,1,0:T(1,128)}), f32[256,1,128]{2,1,0:T(1,128)S(1)}, u32[]{:S(2)}, u32[]{:S(2)}) async-start(f32[256,1,128]{2,1,0:T(1,128)} %bitcast.9), calls=%async_computation.3 | async-start | bytes 262144 | tf_op jit(solution)/shard_map/all_to_all | solution.py:401

commit v6 on v5

--- a/solution.py
+++ b/solution.py
@@ -252,7 +252,7 @@
             moments_ref[which, 0, k : k + 1] = jnp.sum(value * factor, axis=0, keepdims=True)
 
 
-def edge_body(cols, length_x_ref, got_ref, fy_ref, level_ref, moments_ref, out_ref, sum_ref, lhs_ref):
+def edge_body(cols, length_x_ref, got_ref, fy_ref, moments_ref, out_ref, sum_ref, lhs_ref):
     bands, _, lanes = got_ref.shape
     _, levels, members, ny = out_ref.shape
     rows = lanes // members
@@ -262,7 +262,8 @@
         lhs_ref[k : k + 1, :] = piece[0:1]
         lhs_ref[members + k : members + k + 1, :] = piece[1:2]
     lhs = lhs_ref[...]
-    level_of = level_ref[0:1, :]
+    spot = iota((1, bands * rows), 1).astype(F32) + 0.5
+    level_of = (spot * (levels / rows)).astype(jnp.int32) & (levels - 1)
     lhs = jnp.concatenate([jnp.where(level_of == level, lhs, 0.0).astype(BF16) for level in range(levels)], axis=0)
     edge = jnp.dot(lhs, fy_ref[...], preferred_element_type=F32)
     total = jnp.zeros((members, ny), F32)
@@ -386,10 +387,9 @@
 
     _, near, moments = lax.while_loop(lambda carry: carry[0] < rounds[0], again, (jnp.int32(1), near, moments))
 
-    level_of = jnp.broadcast_to(jnp.arange(bands * rows, dtype=jnp.int32) // ny_loc % levels, (8, bands * rows))
     edge, partial_value = pl.pallas_call(
         lambda *refs: edge_body(x_block, *refs),
-        in_specs=[SMEM] + [pl.BlockSpec(memory_space=pltpu.VMEM)] * 4,
+        in_specs=[SMEM] + [pl.BlockSpec(memory_space=pltpu.VMEM)] * 3,
         out_shape=[
             jax.ShapeDtypeStruct((2, levels, members, ny), F32),
             jax.ShapeDtypeStruct((groups * bands, 128), F32),
@@ -397,7 +397,7 @@
         scratch_shapes=[pltpu.VMEM((2 * members, bands * rows), F32)],
         compiler_params=room(16),
         name="edge",
-    )(length_x, edges, filter_y, level_of, moments)
+    )(length_x, edges, filter_y, moments)
     partials = lax.all_to_all(partial_value, ("mem", "band"), 0, 0, tiled=True)
 
     part = 8

time: 87 us -> 87 us (level)
  no operation moved by 1% of the time
where the time goes in v6:
time: 87 us; the launch traced here: 86.6 us
  starting transfers between devices  35.8 us (41%)
  Pallas kernels  29.9 us (34%)
  waiting for transfers between devices  16.7 us (19%)
  between operations  2.55 us (3%)
  loops' own time  0.92 us (1%)
    all_to_all x1, starting transfers between devices, on_device(): partials = lax.all_to_all(partial_value, ('mem', 'band'), 0, 0, tiled=True)  14.9 us
    pallas_call x1, Pallas kernels, near_field(): pl.pallas_call(lambda *refs: near_body(ny_loc, nx, *refs), grid=(levels,)...  12.8 us
    all_to_all x1, starting transfers between devices, route(): got = lax.all_to_all(packed, 'band', 0, 0, tiled=True)  12 us
    all_to_all x1, waiting for transfers between devices, on_device(): partials = lax.all_to_all(partial_value, ('mem', 'band'), 0, 0, tiled=True)  8.78 us
    all_to_all x1, waiting for transfers between devices, route(): got = lax.all_to_all(packed, 'band', 0, 0, tiled=True)  7.92 us
    all_to_all x1, starting transfers between devices, on_device(): edges = lax.all_to_all(states, 'band', 0, 0, tiled=True)  7.05 us
    pallas_call x1, Pallas kernels, on_device(): pl.pallas_call(final_body, grid=(members // part,), in_specs=[SMEM, pl.Bl...  4.24 us
    pallas_call x1, Pallas kernels, route(): pl.pallas_call(lambda *refs: bucket_body(nx, rows, x_block, *refs), in_sp...  4 us
  transfers between devices with their start and end apart: 4, of which 2 were waited for; matrix products, arithmetic and copies ran while one was open for 0% of the time, Pallas kernels for 27%

profile of v6, /device:TPU:1, one launch (start us, length us, event | category | flops | bytes accessed | tf_op | source)
XLA Modules:
  0.0 86.6 jit_solution(3678979206712309788)
XLA Ops:
  0.6 4.0 %bucket.2 = bf16[32,40,128]{2,1,0:T(8,128)(2,1)} custom-call(s32[1]{0:T(128)} %constant.0.clone.1.refs_0_, s32[1,2048]{1,0:T(1,128)} %bitcast.22, s32[1,2048]{1,0:T(1,128)} %bitcast.24, f32[1,2048]{1,0:T(1,128)} %bitcast.26, bf16[16,2048]{1,0:T(8,128)(2,1)} %refs_4_.2), custom_call_target="tpu_custom_call" | custom-call | tf_op jit(solution)/shard_map/bucket/pallas_call | solution.py:306
  4.6 12.0 %all-to-all-start.1 = ((bf16[32,40,128]{2,1,0:T(8,128)(2,1)}), bf16[32,40,128]{2,1,0:T(8,128)(2,1)S(1)}, u32[]{:S(2)}, u32[]{:S(2)}) async-start(bf16[32,40,128]{2,1,0:T(8,128)(2,1)} %bucket.2), calls=%async_computation.1 | async-start | bytes 655360 | tf_op jit(solution)/shard_map/all_to_all | solution.py:318
  16.7 2.2 %filter.1.refs_2_ = bf16[1536,768]{1,0:T(8,128)(2,1)S(1)} custom-call(f32[2]{0:T(128)} %refs_1_.1), custom_call_target="tpu_custom_call" | custom-call | flops 5000000 | bytes 3000000 | tf_op jit(solution)/shard_map/filter/pallas_call | solution.py:359
  18.9 7.9 %all-to-all-done.1.refs_1_ = bf16[32,40,128]{2,1,0:T(8,128)(2,1)S(1)} async-done(((bf16[32,40,128]{2,1,0:T(8,128)(2,1)}), bf16[32,40,128]{2,1,0:T(8,128)(2,1)S(1)}, u32[]{:S(2)}, u32[]{:S(2)}) %all-to-all-start.1) | async-done | bytes 327712 | tf_op jit(solution)/shard_map/all_to_all | solution.py:318
  26.9 1.9 %collective-permute-start.1 = (bf16[32,24,128]{2,1,0:T(8,128)(2,1)S(1)}, bf16[32,24,128]{2,1,0:T(8,128)(2,1)S(1)}, u32[]{:S(2)}, u32[]{:S(2)}) collective-permute-start(bf16[32,24,128]{2,1,0:T(8,128)(2,1)S(1)} %slice.9.refs_2_), channel_id=1, source_target_pairs={{0,16},{1,17},{2,18},{3,19},{4,20},{5,21},{6,22},{7,23},{8,24},{9,... | collective-permute-start | bytes 589832 | tf_op jit(solution)/shard_map/ppermute | solution.py:323
  28.7 3.8 %states.1 = bf16[32,2,768]{2,1,0:T(2,128)(2,1)} custom-call(f32[2]{0:T(128)} %length_x_ref.1, bf16[32,40,128]{2,1,0:T(8,128)(2,1)S(1)} %all-to-all-done.1.refs_1_), custom_call_target="tpu_custom_call" | custom-call | tf_op jit(solution)/shard_map/states/pallas_call | solution.py:371
  32.6 7.1 %all-to-all-start.2 = ((bf16[32,2,768]{2,1,0:T(2,128)(2,1)}), bf16[32,2,768]{2,1,0:T(2,128)(2,1)S(1)}, u32[]{:S(2)}, u32[]{:S(2)}) async-start(bf16[32,2,768]{2,1,0:T(2,128)(2,1)} %states.1), calls=%async_computation.2 | async-start | bytes 196608 | tf_op jit(solution)/shard_map/all_to_all | solution.py:379
  39.6 0.0 copy-start
  39.6 0.0 copy-start.1
  39.7 0.0 copy-start.2
  39.7 0.0 copy-start.3
  39.7 0.0 copy-start.4
  39.7 0.0 copy-start.5
  39.7 0.0 collective-permute-done.1.refs_3_
  39.7 12.8 %near.2 = (f32[16,2,48,768]{3,2,1,0:T(8,128)}, f32[3,2,16,768]{3,2,1,0:T(8,128)}, s32[1]{0:T(128)}) custom-call(f32[2]{0:T(128)} %length_x_ref.1, f32[2]{0:T(128)} %refs_1_.1, bf16[32,24,128]{2,1,0:T(8,128)(2,1)S(1)} %slice.9.refs_2_, bf16[32,24,128]{2,1,0:T(8,128)(2,1)S(1)} %collective-permute-done.1.refs_3_, bf16[16,2,48,768]{3,2,1,0:T(8,128)(2,1)} %refs_4_.3), custom_call_target="tpu_custom_call" | custom-call | flops 4831838208 | bytes 8000000 | tf_op jit(solution)/shard_map/near/pallas_call | solution.py:328
  52.5 0.0 all-to-all-done.2.refs_1_
  52.5 0.0 copy-done
  52.5 0.0 copy-done.1
  52.6 0.0 copy-done.2
  52.6 0.0 copy-done.3
  52.6 0.0 copy-done.4
  52.6 0.0 copy-done.5
  52.6 0.9 %while.12 = (s32[]{:T(128)}, f32[16,2,48,768]{3,2,1,0:T(8,128)}, f32[3,2,16,768]{3,2,1,0:T(8,128)}, s32[1]{0:T(128)}, s32[2048,1]{0,1:T(1,128)S(1)}, /*index=5*/...) while((s32[]{:T(128)}, f32[16,2,48,768]{3,2,1,0:T(8,128)}, ...), condition=%wide.region_1.0_spmd, body=%wide.region_0.0_spmd.sunk | while | flops 4831838208 | bytes 19272340 | solution.py:388
  53.5 2.7 %edge.1 = (f32[2,2,16,768]{3,2,1,0:T(8,128)S(1)}, f32[256,128]{1,0:T(8,128)}) custom-call(f32[2]{0:T(128)S(1)} %get-tuple-element.197, bf16[32,2,768]{2,1,0:T(2,128)(2,1)S(1)} %all-to-all-done.2.refs_1_, bf16[1536,768]{1,0:T(8,128)(2,1)S(1)} %filter.1.refs_2_, f32[3,2,16,768]{3,2,1,0:T(8,128)} %get-tuple-element.69.refs_3_), custom_call_target="tpu_custom_call" | custom-call | tf_op jit(solution)/shard_map/edge/pallas_call | solution.py:390
  56.3 14.9 %all-to-all-start.3 = ((f32[256,1,128]{2,1,0:T(1,128)}), f32[256,1,128]{2,1,0:T(1,128)S(1)}, u32[]{:S(2)}, u32[]{:S(2)}) async-start(f32[256,1,128]{2,1,0:T(1,128)} %bitcast.9), calls=%async_computation.3 | async-start | bytes 262144 | tf_op jit(solution)/shard_map/all_to_all | solution.py:401
  71.1 4.2 %final.1 = f32[16,2,48,768]{3,2,1,0:T(8,128)} custom-call(f32[2]{0:T(128)S(1)} %get-tuple-element.197, f32[2,2,16,768]{3,2,1,0:T(8,128)S(1)} %get-tuple-element.70.edge_ref, f32[16,2,48,768]{3,2,1,0:T(8,128)} %get-tuple-element.71.near_ref), custom_call_target="tpu_custom_call" | custom-call | flops 20000000 | bytes 10000000 | tf_op jit(solution)/shard_map/final/pallas_call | solution.py:405
  75.4 8.8 %all-to-all-done.3 = f32[256,1,128]{2,1,0:T(1,128)S(1)} async-done(((f32[256,1,128]{2,1,0:T(1,128)}), f32[256,1,128]{2,1,0:T(1,128)S(1)}, u32[]{:S(2)}, u32[]{:S(2)}) %all-to-all-start.3) | async-done | bytes 131104 | tf_op jit(solution)/shard_map/all_to_all | solution.py:401
  84.2 0.6 slice_reduce_fusion
  (1 shorter events, 0.0 us)
Async XLA Ops:
  4.6 22.2 %all-to-all-start.1 = ((bf16[32,40,128]{2,1,0:T(8,128)(2,1)}), bf16[32,40,128]{2,1,0:T(8,128)(2,1)S(1)}, u32[]{:S(2)}, u32[]{:S(2)}) async-start(bf16[32,40,128]{2,1,0:T(8,128)(2,1)} %bucket.2), calls=%async_computation.1 | async-start | bytes 655360 | tf_op jit(solution)/shard_map/all_to_all | solution.py:318
  26.9 12.8 %collective-permute-start.1 = (bf16[32,24,128]{2,1,0:T(8,128)(2,1)S(1)}, bf16[32,24,128]{2,1,0:T(8,128)(2,1)S(1)}, u32[]{:S(2)}, u32[]{:S(2)}) collective-permute-start(bf16[32,24,128]{2,1,0:T(8,128)(2,1)S(1)} %slice.9.refs_2_), channel_id=1, source_target_pairs={{0,16},{1,17},{2,18},{3,19},{4,20},{5,21},{6,22},{7,23},{8,24},{9,... | collective-permute-start | bytes 589832 | tf_op jit(solution)/shard_map/ppermute | solution.py:323
  32.6 20.0 %all-to-all-start.2 = ((bf16[32,2,768]{2,1,0:T(2,128)(2,1)}), bf16[32,2,768]{2,1,0:T(2,128)(2,1)S(1)}, u32[]{:S(2)}, u32[]{:S(2)}) async-start(bf16[32,2,768]{2,1,0:T(2,128)(2,1)} %states.1), calls=%async_computation.2 | async-start | bytes 196608 | tf_op jit(solution)/shard_map/all_to_all | solution.py:379
  39.6 12.9 %copy-start = (bf16[16,2048]{1,0:T(8,128)(2,1)S(1)}, bf16[16,2048]{1,0:T(8,128)(2,1)}, u32[]{:S(2)}) copy-start(bf16[16,2048]{1,0:T(8,128)(2,1)} %refs_4_.2) | copy-start | bytes 196612
  39.6 12.9 %copy-start.1 = (s32[2048,1]{0,1:T(1,128)S(1)}, s32[2048,1]{0,1:T(1,128)}, u32[]{:S(2)}) copy-start(s32[2048,1]{0,1:T(1,128)} %param.12) | copy-start | bytes 24580
  39.7 12.9 %copy-start.2 = (s32[2048]{0:T(1024)S(1)}, s32[2048]{0:T(1024)}, u32[]{:S(2)}) copy-start(s32[2048]{0:T(1024)} %param.13) | copy-start | bytes 24580
  39.7 12.9 %copy-start.3 = (f32[2048]{0:T(1024)S(1)}, f32[2048]{0:T(1024)}, u32[]{:S(2)}) copy-start(f32[2048]{0:T(1024)} %param.11) | copy-start | bytes 24580
  39.7 12.9 %copy-start.4 = (f32[2]{0:T(128)S(1)}, f32[2]{0:T(128)}, u32[]{:S(2)}) copy-start(f32[2]{0:T(128)} %length_x_ref.1) | copy-start | bytes 28
  39.7 12.9 %copy-start.5 = (f32[2]{0:T(128)S(1)}, f32[2]{0:T(128)}, u32[]{:S(2)}) copy-start(f32[2]{0:T(128)} %refs_1_.1) | copy-start | bytes 28
  56.3 27.9 %all-to-all-start.3 = ((f32[256,1,128]{2,1,0:T(1,128)}), f32[256,1,128]{2,1,0:T(1,128)S(1)}, u32[]{:S(2)}, u32[]{:S(2)}) async-start(f32[256,1,128]{2,1,0:T(1,128)} %bitcast.9), calls=%async_computation.3 | async-start | bytes 262144 | tf_op jit(solution)/shard_map/all_to_all | solution.py:401
